TPU v7x, 256 devices: a whole 4x4x8 slice. The times are simulated.
256 devices in a mesh: ctx: 8 (over y, core), head: 32 (over x, z).
Axes of the slice: x: 4, y: 4, z: 8, core: 2. Of those that a mesh axis runs over, the one named last changes fastest.
Arguments:
- queries: bfloat16 [32768, 4096], P('ctx', 'head'), may hold values from -24 to 24
- win_key: bfloat16 [32768, 1024], P(('ctx', 'head')), may hold values from -24 to 24
- win_value: bfloat16 [32768, 1024], P(('ctx', 'head')), may hold values from -6 to 6
- past_key: bfloat16 [524288, 1024], P(('ctx', 'head')), may hold values from -24 to 24
- past_value: bfloat16 [524288, 1024], P(('ctx', 'head')), may hold values from -6 to 6
- chosen: int32 [256, 32, 3], P('ctx', 'head'), may hold values from 0 to 1023, as said below
Outputs:
- attended: bfloat16 [32768, 4096], P('ctx', 'head')
Inputs may be any that keep to these rules, and one draw needn't show every extreme that they name: `chosen`: block b of the cache is held by the device of linear index b // 4, counted over ctx then head. Of the entries held by one device (its query blocks and its heads), at most 1 fall on any one owner, and one owner receives exactly 1 from every device. The 3 blocks of one list lie on distinct owners.
All inputs are finite; a program needn't handle non-finite values.
Results may differ from a plain program's by a relative error of at most 0.019.
Values may be sent and summed in bfloat16 or wider, within the bound.
No kernel may reach another device: no remote copies, remote signals or barrier semaphores. Data moves between devices by JAX's collectives and lax.ppermute only.
A program may use at most 128 MiB of HBM per device.

v0:
```python
from functools import partial
import math

import jax
import jax.numpy as jnp
import numpy as np
from jax import lax
from jax.sharding import PartitionSpec as P

HEADS = 32
KVH = 8
DH = 128
BLK = 512
QBLK = 128
TOPK = 3


def shortened(x):
    return jax.tree.map(lambda a: a.astype(jnp.bfloat16) if a.dtype == jnp.float32 else a, x)


def own_block(operands, kv_local, group_width, scale_factor):
    query_block, key_block, value_block = operands
    rows_here = query_block.shape[0]
    grouped = query_block.reshape(rows_here, kv_local, group_width, DH)
    scores = (
        jnp.einsum("ikgd,tkd->kgit", grouped, key_block, preferred_element_type=jnp.float32)
        * scale_factor
    )
    positions = jnp.arange(rows_here)
    causal = positions[None, :] <= positions[:, None]
    scores = jnp.where(causal, scores, -jnp.inf)
    row_max = jnp.max(scores, axis=-1)
    softmax_terms = jnp.exp(scores - row_max[..., None])
    row_total = jnp.sum(softmax_terms, axis=-1)
    output = jnp.einsum(
        "kgit,tkd->ikgd",
        softmax_terms.astype(jnp.bfloat16),
        value_block,
        preferred_element_type=jnp.float32,
    )
    heads_here = kv_local * group_width
    return (
        output.reshape(rows_here, heads_here, DH),
        row_max.reshape(heads_here, rows_here).T,
        row_total.reshape(heads_here, rows_here).T,
    )


def far_slots(operands, past_keys, past_values, scale_factor):
    query_group, meta_group = operands
    valid_meta = jnp.maximum(meta_group, 0)
    block_local = valid_meta // KVH
    kv_index = valid_meta % KVH
    key_tiles = past_keys[block_local, :, kv_index, :]
    value_tiles = past_values[block_local, :, kv_index, :]
    scores = (
        jnp.einsum("gqd,gtd->gqt", query_group, key_tiles, preferred_element_type=jnp.float32)
        * scale_factor
    )
    row_max = jnp.max(scores, axis=-1)
    softmax_terms = jnp.exp(scores - row_max[..., None])
    row_total = jnp.sum(softmax_terms, axis=-1)
    output = jnp.einsum(
        "gqt,gtd->gqd",
        softmax_terms.astype(jnp.bfloat16),
        value_tiles,
        preferred_element_type=jnp.float32,
    )
    return (output.astype(jnp.bfloat16), row_max, row_total)


def shards(queries, win_key, win_value, past_key, past_value, chosen):
    ctx_count = lax.axis_size("ctx")
    head_count = lax.axis_size("head")
    device_count = ctx_count * head_count
    head_local = HEADS // head_count
    group_size = HEADS // KVH
    kv_local = max(1, head_local // group_size)
    group_width = head_local // kv_local
    scale_factor = 1.0 / math.sqrt(DH)
    query_rows = queries.shape[0]
    window_local = win_key.shape[0]
    head_index = lax.axis_index("head")
    kv_table = (
        np.arange(head_count)[:, None] * head_local // group_size + np.arange(kv_local)[None, :]
    ).reshape(-1)
    key_pieces = win_key.reshape(window_local, KVH, DH)[:, kv_table, :].reshape(
        window_local, head_count, kv_local * DH
    )
    value_pieces = win_value.reshape(window_local, KVH, DH)[:, kv_table, :].reshape(
        window_local, head_count, kv_local * DH
    )
    own_keys, own_values = (
        lax.all_to_all(key_pieces, "head", split_axis=1, concat_axis=0, tiled=True),
        lax.all_to_all(value_pieces, "head", split_axis=1, concat_axis=0, tiled=True),
    )
    own_keys = own_keys.reshape(query_rows // BLK, BLK, kv_local, DH)
    own_values = own_values.reshape(query_rows // BLK, BLK, kv_local, DH)
    query_blocks = queries.reshape(query_rows // BLK, BLK, head_local, DH)
    list_ids = chosen.reshape(-1)
    request_count = list_ids.shape[0]
    blocks_local = past_key.shape[0] // BLK
    capacity = -(-request_count // device_count)
    slot_count = device_count * capacity
    owners = list_ids // blocks_local
    block_local = list_ids % blocks_local
    matches = (owners[:, None] == jnp.arange(device_count, dtype=jnp.int32)[None, :]).astype(
        jnp.int32
    )
    rank_within = jnp.sum(jnp.cumsum(matches, axis=0) * matches, axis=1) - 1
    slot_of = owners * capacity + rank_within
    request_iota = jnp.arange(request_count, dtype=jnp.int32)
    head_of = request_iota // TOPK % head_local
    block_of = request_iota // (TOPK * head_local)
    kv_of = (head_index * head_local + head_of) // group_size
    meta_of = block_local * KVH + kv_of
    query_tiles = queries.reshape(query_rows // QBLK, QBLK, head_local, DH)[block_of, :, head_of, :]
    send_tiles = jnp.zeros((slot_count, QBLK, DH), jnp.bfloat16).at[slot_of].set(query_tiles)
    send_tiles = send_tiles.reshape(ctx_count, head_count, capacity, QBLK, DH)
    send_meta = jnp.full((slot_count,), -1, jnp.int32).at[slot_of].set(meta_of)
    send_meta = send_meta.reshape(ctx_count, head_count, capacity)
    got_tiles, got_meta = (
        lax.all_to_all(
            lax.all_to_all(send_tiles, "ctx", split_axis=0, concat_axis=0, tiled=True),
            "head",
            split_axis=1,
            concat_axis=1,
            tiled=True,
        ),
        lax.all_to_all(
            lax.all_to_all(send_meta, "ctx", split_axis=0, concat_axis=0, tiled=True),
            "head",
            split_axis=1,
            concat_axis=1,
            tiled=True,
        ),
    )
    own_out, own_max, own_total = lax.map(
        partial(own_block, kv_local=kv_local, group_width=group_width, scale_factor=scale_factor),
        (query_blocks, own_keys, own_values),
    )
    own_out = own_out.reshape(query_rows, head_local, DH)
    own_max = own_max.reshape(query_rows, head_local)
    own_total = own_total.reshape(query_rows, head_local)
    turn_count = 16
    per_turn = slot_count // turn_count
    past_keys = past_key.reshape(blocks_local, BLK, KVH, DH)
    past_values = past_value.reshape(blocks_local, BLK, KVH, DH)
    slot_out, slot_max, slot_total = lax.map(
        partial(far_slots, past_keys=past_keys, past_values=past_values, scale_factor=scale_factor),
        (got_tiles.reshape(turn_count, per_turn, QBLK, DH), got_meta.reshape(turn_count, per_turn)),
    )
    slot_out = slot_out.reshape(ctx_count, head_count, capacity, QBLK, DH)
    slot_max = slot_max.reshape(ctx_count, head_count, capacity, QBLK)
    slot_total = slot_total.reshape(ctx_count, head_count, capacity, QBLK)
    back_out, back_max, back_total = (
        lax.all_to_all(
            lax.all_to_all(shortened(slot_out), "ctx", split_axis=0, concat_axis=0, tiled=True),
            "head",
            split_axis=1,
            concat_axis=1,
            tiled=True,
        ).astype(slot_out.dtype),
        lax.all_to_all(
            lax.all_to_all(shortened(slot_max), "ctx", split_axis=0, concat_axis=0, tiled=True),
            "head",
            split_axis=1,
            concat_axis=1,
            tiled=True,
        ).astype(slot_max.dtype),
        lax.all_to_all(
            lax.all_to_all(shortened(slot_total), "ctx", split_axis=0, concat_axis=0, tiled=True),
            "head",
            split_axis=1,
            concat_axis=1,
            tiled=True,
        ).astype(slot_total.dtype),
    )
    block_count = query_rows // QBLK
    far_out = back_out.reshape(slot_count, QBLK, DH)[slot_of].reshape(
        block_count, head_local, TOPK, QBLK, DH
    )
    far_max = back_max.reshape(slot_count, QBLK)[slot_of].reshape(
        block_count, head_local, TOPK, QBLK
    )
    far_total = back_total.reshape(slot_count, QBLK)[slot_of].reshape(
        block_count, head_local, TOPK, QBLK
    )
    own_out_t = own_out.reshape(block_count, QBLK, head_local, DH).transpose(0, 2, 1, 3)
    own_max_t = own_max.reshape(block_count, QBLK, head_local).transpose(0, 2, 1)
    own_total_t = own_total.reshape(block_count, QBLK, head_local).transpose(0, 2, 1)
    top_score = jnp.maximum(own_max_t, jnp.max(far_max, axis=2))
    own_weight = jnp.exp(own_max_t - top_score)
    far_weight = jnp.exp(far_max - top_score[:, :, None])
    total_weight = own_total_t * own_weight + jnp.sum(far_total * far_weight, axis=2)
    numerator = own_out_t * own_weight[..., None] + jnp.sum(
        far_out.astype(jnp.float32) * far_weight[..., None], axis=2
    )
    merged = numerator / total_weight[..., None]
    return merged.transpose(0, 2, 1, 3).reshape(query_rows, head_local * DH).astype(jnp.bfloat16)


def solution(mesh):
    return jax.shard_map(
        shards,
        mesh=mesh,
        in_specs=(
            P("ctx", "head"),
            P(("ctx", "head"), None),
            P(("ctx", "head"), None),
            P(("ctx", "head"), None),
            P(("ctx", "head"), None),
            P("ctx", "head", None),
        ),
        out_specs=P("ctx", "head"),
        check_vma=False,
    )
```

profile of v0, /device:TPU:1, one launch (start us, length us, event | category | flops | bytes accessed | tf_op | source)
XLA Modules:
  0.0 1010.8 jit_solution(1004859677671878973)
XLA Ops:
  3.0 6.5 all-to-all-start.4
  12.0 5.4 broadcast_in_dim.80
  17.3 12.8 %scatter_fusion = bf16[256,128,128]{2,1,0:T(8,128)(2,1)} fusion(bf16[256,128,128]{2,1,0:T(8,128)(2,1)} %broadcast_in_dim.80, s32[96]{0:T(128)S(1)} %fusion.53, bf16[96,128,128]{2,1,0:T(8,128)(2,1)S(1)} %gather_fusion.4), kind=kCustom, calls=%fused_computation.8 | custom fusion | bytes 9437568 | tf_op jit(solution)/shard_map/scatter | solution.py:119
  30.1 4.9 all-to-all-start.2
  35.8 93.2 %all-to-all-done.2 = bf16[8,32,1,128,128]{4,3,1,2,0:T(8,128)(2,1)} async-done(((bf16[8,32,1,128,128]{4,3,1,2,0:T(8,128)(2,1)}), bf16[8,32,1,128,128]{4,3,1,2,0:T(8,128)(2,1)}, u32[]{:S(2)}, u32[]{:S(2)}) %all-to-all-start.2) | async-done | bytes 8388640 | tf_op jit(solution)/shard_map/all_to_all | solution.py:125
  128.9 10.6 %all-to-all-start.5 = ((s32[8,32,1]{0,2,1:T(1,128)}), s32[8,32,1]{0,2,1:T(1,128)S(1)}, u32[]{:S(2)}, u32[]{:S(2)}) async-start(s32[8,32,1]{0,2,1:T(1,128)} %copy.64), calls=%async_computation.5 | async-start | bytes 32768 | tf_op jit(solution)/shard_map/all_to_all | solution.py:131
  139.5 10.3 %copy.62 = bf16[8,32,1,128,128]{4,3,0,2,1:T(8,128)(2,1)} copy(bf16[8,32,1,128,128]{4,3,1,2,0:T(8,128)(2,1)} %all-to-all-done.2) | data formatting | bytes 16777216 | tf_op jit(solution)/shard_map/all_to_all | solution.py:125
  149.9 9.5 all-to-all-start.3
  161.4 180.8 %all-to-all-done.3 = bf16[8,32,1,128,128]{4,3,0,2,1:T(8,128)(2,1)} async-done(((bf16[8,32,1,128,128]{4,3,0,2,1:T(8,128)(2,1)}), bf16[8,32,1,128,128]{4,3,0,2,1:T(8,128)(2,1)}, u32[]{:S(2)}, u32[]{:S(2)}) %all-to-all-start.3) | async-done | bytes 8388640 | tf_op jit(solution)/shard_map/all_to_all | solution.py:124
  342.2 14.7 %all-to-all-start = ((bf16[128,32,128]{2,0,1:T(8,128)(2,1)}), bf16[128,32,128]{2,0,1:T(8,128)(2,1)S(1)}, u32[]{:S(2)}, u32[]{:S(2)}) async-start(bf16[128,32,128]{2,0,1:T(8,128)(2,1)} %bitcast.20), calls=%async_computation | async-start | bytes 2097152 | tf_op jit(solution)/shard_map/all_to_all | solution.py:96
  369.3 10.3 %copy.63 = bf16[8,32,1,128,128]{4,3,1,0,2:T(8,128)(2,1)} copy(bf16[8,32,1,128,128]{4,3,0,2,1:T(8,128)(2,1)} %all-to-all-done.3) | data formatting | bytes 16777216 | tf_op jit(solution)/shard_map/all_to_all | solution.py:124
  381.8 8.3 all-to-all-start.1
  390.1 256.4 %while.31 = (s32[]{:T(128)}, bf16[16,16,128,128]{3,2,1,0:T(8,128)(2,1)}, bf16[16,16,128]{2,1,0:T(8,128)(2,1)S(1)}, bf16[16,16,128]{2,1,0:T(8,128)(2,1)}, bf16[16...) while((s32[]{:T(128)}, ...), condition=%wide.region_11.12_spmd, body=%wide.region_8.11_spmd.sunk | while | flops 545517952 | bytes 43046912 | solution.py:150
  400.1 4.1 fusion.78
  416.2 4.1 fusion.78
  464.2 4.1 fusion.78
  528.3 4.1 fusion.78
  544.3 4.1 fusion.78
  592.4 4.1 fusion.78
  608.4 4.1 fusion.78
  640.5 4.1 fusion.78
  646.5 9.5 all_to_all.80
  660.1 4.8 all-to-all-done.10
  664.9 18.1 %all_to_all.81 = bf16[8,32,1,128]{3,0,2,1:T(8,128)(2,1)S(1)} all-to-all(bf16[8,32,1,128]{3,0,2,1:T(8,128)(2,1)S(1)} %copy.68), channel_id=1, replica_groups=mesh['ctx'=8,'head'=32] {'head'}, dimensions={1} | all-to-all | bytes 131072 | tf_op jit(solution)/shard_map/all_to_all | solution.py:165
  683.0 7.0 all-to-all-start.8
  690.7 93.2 %all-to-all-done.8 = bf16[8,32,1,128,128]{4,3,1,2,0:T(8,128)(2,1)} async-done(((bf16[8,32,1,128,128]{4,3,1,2,0:T(8,128)(2,1)}), bf16[8,32,1,128,128]{4,3,1,2,0:T(8,128)(2,1)}, u32[]{:S(2)}, u32[]{:S(2)}) %all-to-all-start.8) | async-done | bytes 8388640 | tf_op jit(solution)/shard_map/all_to_all | solution.py:159
  788.0 10.3 %copy.70 = bf16[8,32,1,128,128]{4,3,0,2,1:T(8,128)(2,1)} copy(bf16[8,32,1,128,128]{4,3,1,2,0:T(8,128)(2,1)} %all-to-all-done.8) | data formatting | bytes 16777216 | tf_op jit(solution)/shard_map/all_to_all | solution.py:159
  798.3 9.1 all-to-all-start.9
  807.5 21.5 %while.30 = (s32[]{:T(128)}, f32[8,512,1,128]{3,1,0,2:T(8,128)}, f32[8,512,1]{1,2,0:T(1,128)S(1)}, f32[8,512,1]{1,2,0:T(1,128)S(1)}, bf16[8,512,1,128]{3,1,2,0:T...) while((s32[]{:T(128)}, f32[8,512,1,128]{3,1,0,2:T(8,128)}, ...), condition=%wide.region_3.4_spmd, body=%wide.region_0.3_spmd.sunk | while | flops 136313856 | bytes 4867677 | solution.py:139
  830.6 160.0 %all-to-all-done.9 = bf16[8,32,1,128,128]{4,3,0,2,1:T(8,128)(2,1)} async-done(((bf16[8,32,1,128,128]{4,3,0,2,1:T(8,128)(2,1)}), bf16[8,32,1,128,128]{4,3,0,2,1:T(8,128)(2,1)}, u32[]{:S(2)}, u32[]{:S(2)}) %all-to-all-start.9) | async-done | bytes 8388640 | tf_op jit(solution)/shard_map/all_to_all | solution.py:158
  990.6 10.3 %copy.71 = bf16[8,32,1,128,128]{4,3,1,0,2:T(8,128)(2,1)} copy(bf16[8,32,1,128,128]{4,3,0,2,1:T(8,128)(2,1)} %all-to-all-done.9) | data formatting | bytes 16777216 | tf_op jit(solution)/shard_map/all_to_all | solution.py:158
  1001.0 4.5 gather_fusion.6
  (266 shorter events, 282.4 us)
Async XLA Ops:
  3.0 27.1 %all-to-all-start.4 = ((s32[8,32,1]{1,2,0:T(1,128)}), s32[8,32,1]{1,2,0:T(1,128)S(1)}, u32[]{:S(2)}, u32[]{:S(2)}) async-start(s32[8,32,1]{1,2,0:T(1,128)} %reshape.529), calls=%async_computation.4 | async-start | bytes 8192 | tf_op jit(solution)/shard_map/all_to_all | solution.py:132
  30.1 98.8 %all-to-all-start.2 = ((bf16[8,32,1,128,128]{4,3,1,2,0:T(8,128)(2,1)}), bf16[8,32,1,128,128]{4,3,1,2,0:T(8,128)(2,1)}, u32[]{:S(2)}, u32[]{:S(2)}) async-start(bf16[8,32,1,128,128]{4,3,1,2,0:T(8,128)(2,1)} %bitcast.169), calls=%async_computation.2 | async-start | bytes 16777216 | tf_op jit(solution)/shard_map/all_to_all | solution.py:125
  128.9 20.9 %all-to-all-start.5 = ((s32[8,32,1]{0,2,1:T(1,128)}), s32[8,32,1]{0,2,1:T(1,128)S(1)}, u32[]{:S(2)}, u32[]{:S(2)}) async-start(s32[8,32,1]{0,2,1:T(1,128)} %copy.64), calls=%async_computation.5 | async-start | bytes 32768 | tf_op jit(solution)/shard_map/all_to_all | solution.py:131
  149.9 9.5 copy-start.3
  149.9 9.9 copy-start.5
  149.9 192.3 %all-to-all-start.3 = ((bf16[8,32,1,128,128]{4,3,0,2,1:T(8,128)(2,1)}), bf16[8,32,1,128,128]{4,3,0,2,1:T(8,128)(2,1)}, u32[]{:S(2)}, u32[]{:S(2)}) async-start(bf16[8,32,1,128,128]{4,3,0,2,1:T(8,128)(2,1)} %copy.62), calls=%async_computation.3 | async-start | bytes 16777216 | tf_op jit(solution)/shard_map/all_to_all | solution.py:124
  342.2 39.6 %all-to-all-start = ((bf16[128,32,128]{2,0,1:T(8,128)(2,1)}), bf16[128,32,128]{2,0,1:T(8,128)(2,1)S(1)}, u32[]{:S(2)}, u32[]{:S(2)}) async-start(bf16[128,32,128]{2,0,1:T(8,128)(2,1)} %bitcast.20), calls=%async_computation | async-start | bytes 2097152 | tf_op jit(solution)/shard_map/all_to_all | solution.py:96
  360.2 2.9 copy-start.1
  364.3 2.9 copy-start.4
  381.8 264.7 %all-to-all-start.1 = ((bf16[128,32,128]{2,0,1:T(8,128)(2,1)}), bf16[128,32,128]{2,0,1:T(8,128)(2,1)}, u32[]{:S(2)}, u32[]{:S(2)}) async-start(bf16[128,32,128]{2,0,1:T(8,128)(2,1)} %bitcast.26), calls=%async_computation.1 | async-start | bytes 2097152 | tf_op jit(solution)/shard_map/all_to_all | solution.py:95
  400.1 4.2 copy-start
  416.2 4.2 copy-start
  432.2 4.1 copy-start
  448.2 4.1 copy-start
  464.2 4.1 copy-start
  480.3 4.1 copy-start
  496.3 4.1 copy-start
  512.3 4.1 copy-start
  528.3 4.1 copy-start
  544.3 4.1 copy-start
  560.4 4.1 copy-start
  576.4 4.1 copy-start
  592.4 4.1 copy-start
  608.4 4.1 copy-start
  624.5 4.1 copy-start
  640.5 4.1 copy-start
  656.0 8.9 all-to-all-start.10
  683.0 100.9 %all-to-all-start.8 = ((bf16[8,32,1,128,128]{4,3,1,2,0:T(8,128)(2,1)}), bf16[8,32,1,128,128]{4,3,1,2,0:T(8,128)(2,1)}, u32[]{:S(2)}, u32[]{:S(2)}) async-start(bf16[8,32,1,128,128]{4,3,1,2,0:T(8,128)(2,1)} %bitcast.177), calls=%async_computation.8 | async-start | bytes 16777216 | tf_op jit(solution)/shard_map/all_to_all | solution.py:159
  783.9 14.4 %all-to-all-start.11 = ((bf16[8,32,1,128]{3,0,2,1:T(8,128)(2,1)}), bf16[8,32,1,128]{3,0,2,1:T(8,128)(2,1)S(1)}, u32[]{:S(2)}, u32[]{:S(2)}) async-start(bf16[8,32,1,128]{3,0,2,1:T(8,128)(2,1)} %copy.72), calls=%async_computation.11 | async-start | bytes 131072 | tf_op jit(solution)/shard_map/all_to_all | solution.py:172
  798.3 192.3 %all-to-all-start.9 = ((bf16[8,32,1,128,128]{4,3,0,2,1:T(8,128)(2,1)}), bf16[8,32,1,128,128]{4,3,0,2,1:T(8,128)(2,1)}, u32[]{:S(2)}, u32[]{:S(2)}) async-start(bf16[8,32,1,128,128]{4,3,0,2,1:T(8,128)(2,1)} %copy.70), calls=%async_computation.9 | async-start | bytes 16777216 | tf_op jit(solution)/shard_map/all_to_all | solution.py:158
  1005.5 2.1 copy-start.2
where the time goes:
time: 1020 us; the launch traced here: 1010 us
  waiting for transfers between devices  534 us (52%)
  local copies, waits for them, and re-layouts  203 us (20%)
  matrix products  137 us (13%)
  starting transfers between devices  78.7 us (8%)
  other arithmetic  28.4 us (3%)
  blocking collectives  27.6 us (3%)
    all_to_all x1, waiting for transfers between devices, shards(): lax.all_to_all(lax.all_to_all(send_tiles, 'ctx', split_axis=0, concat_axi...  181 us
    all_to_all x1, waiting for transfers between devices, shards(): lax.all_to_all(lax.all_to_all(shortened(slot_out), 'ctx', split_axis=0, c...  160 us
    all_to_all x1, waiting for transfers between devices, shards(): lax.all_to_all(shortened(slot_out), 'ctx', split_axis=0, concat_axis=0, t...  93.2 us
    all_to_all x1, waiting for transfers between devices, shards(): lax.all_to_all(send_tiles, 'ctx', split_axis=0, concat_axis=0, tiled=True)  93.2 us
    dot_general x16, matrix products, far_slots(): jnp.einsum('gqt,gtd->gqd', softmax_terms.astype(jnp.bfloat16), value_tile...  65.6 us
    dot_general x16, matrix products, far_slots(): jnp.einsum('gqd,gtd->gqt', query_group, key_tiles, preferred_element_type...  59 us
    gather x16, local copies, waits for them, and re-layouts, far_slots(): key_tiles = past_keys[block_local, :, kv_index, :]  50.2 us
    gather x16, local copies, waits for them, and re-layouts, far_slots(): value_tiles = past_values[block_local, :, kv_index, :]  50.2 us
  transfers between devices with their start and end apart: 10, of which 6 were waited for; matrix products, arithmetic and copies ran while one was open for 34% of the time, Pallas kernels for 0%

commit v1 on v0

v1 whole, which is shorter than its diff:
```python
import functools
import math

import jax
import jax.numpy as jnp
from jax import lax
from jax.experimental import pallas as pl
from jax.experimental.pallas import tpu as pltpu
from jax.sharding import Mesh, PartitionSpec as P

DH = 128
BLK = 512
QBLK = 128
TOPK = 3
TILES = 32
PLANE = 32
NZ = 8
REQ = 96
UNROLL = 4
EXP_SCALE = math.log2(math.e) / math.sqrt(DH)
NONE = -1e30
BF = jnp.bfloat16
F32 = jnp.float32

VMEM = pl.BlockSpec(memory_space=pltpu.VMEM)
SMEM = pl.BlockSpec(memory_space=pltpu.SMEM)
ANY = pl.BlockSpec(memory_space=pl.ANY)


def params():
    return pltpu.CompilerParams(vmem_limit_bytes=48 * 1024 * 1024)


def mxu(a, b):
    return jnp.dot(a, b, preferred_element_type=F32)


def pack_kernel(aways, stride, idx_ref, *refs):
    n = len(aways)
    sources, out_ref, sem = refs[:n], refs[n], refs[n + 1]

    @pl.loop(0, PLANE)
    def _(owner):
        for j in range(n):
            pltpu.make_async_copy(
                sources[j].at[idx_ref[owner * stride + aways[j]]],
                out_ref.at[owner, pl.ds(j * QBLK, QBLK), :],
                sem,
            ).start()

    pltpu.make_async_copy(out_ref, out_ref, sem).wait()


def pack(sources, aways, idx):
    stride = idx.shape[0] // PLANE
    n = len(sources)
    return pl.pallas_call(
        functools.partial(pack_kernel, aways, stride),
        out_shape=jax.ShapeDtypeStruct((PLANE, n * QBLK, DH), BF),
        in_specs=[SMEM] + [VMEM] * n,
        out_specs=ANY,
        scratch_shapes=[pltpu.SemaphoreType.DMA],
        compiler_params=params(),
        cost_estimate=pl.CostEstimate(
            flops=0, bytes_accessed=2 * n * PLANE * QBLK * DH * 2, transcendentals=0
        ),
        name=f"pack{n}",
    )(idx, *sources)


def far_kernel(
    aways, first, meta_ref, got_ref, k_ref, vt_ref, out_ref, q_ref, lse_ref, list_ref, sem
):
    n = len(aways)
    slots = PLANE * n

    def meta_of(slot):
        if n == 1:
            return meta_ref[slot * NZ + aways[0]]
        return meta_ref[slot // 2 * NZ + jnp.where(slot % 2 == 0, aways[0], aways[1])]

    copy = pltpu.make_async_copy(
        got_ref.at[:, first * QBLK : (first + n) * QBLK, :], q_ref, sem
    )
    copy.start()
    out_ref[...] = jnp.zeros_like(out_ref)
    lse_ref[...] = jnp.zeros_like(lse_ref)

    def listed(i, count):
        list_ref[count] = i
        return count + (meta_of(i) >= 0).astype(jnp.int32)

    count = lax.fori_loop(0, slots, listed, jnp.int32(0))
    last = list_ref[jnp.maximum(count - 1, 0)]
    for u in range(UNROLL):
        list_ref[count + u] = last
    copy.wait()

    @pl.loop(0, (count + UNROLL - 1) // UNROLL)
    def _(turn):
        ids = [list_ref[turn * UNROLL + u] for u in range(UNROLL)]
        scores, values = [], []
        for slot in ids:
            meta = meta_of(slot)
            keys = pl.multiple_of((meta // 8) * BLK, BLK)
            cols = pl.multiple_of((meta % 8) * DH, DH)
            q = q_ref[slot // n, pl.ds(pl.multiple_of(slot % n * QBLK, QBLK), QBLK), :]
            scores.append(mxu(k_ref[pl.ds(keys, BLK), pl.ds(cols, DH)], q))
            values.append(vt_ref[pl.ds(cols, DH), pl.ds(keys, BLK)])
        tops = [jnp.max(s, axis=0, keepdims=True) for s in scores]
        terms = [jnp.exp2((s - m) * EXP_SCALE) for s, m in zip(scores, tops)]
        totals = [jnp.sum(t, axis=0, keepdims=True) for t in terms]
        outs = [mxu(v, t.astype(BF)) for v, t in zip(values, terms)]
        for slot, o, m, l in zip(ids, outs, tops, totals):
            out_ref[slot // n, pl.ds(pl.multiple_of(slot % n * QBLK, QBLK), QBLK), :] = (
                o * (1.0 / l)
            ).astype(BF)
            lse_ref[slot] = m * EXP_SCALE + jnp.log2(l)

    @pl.loop(0, PLANE)
    def _(source):
        rows = []
        for j in range(n):
            rows += split3(lse_ref[source * n + j])
        rows.append(jnp.zeros((16 - len(rows), DH), F32))
        out_ref[source, n * QBLK :, :] = jnp.concatenate(rows, axis=0).astype(BF)


def far(tiles, first, aways, meta, past_key, past_value_t):
    n = len(aways)
    slots = PLANE * n
    return pl.pallas_call(
        functools.partial(far_kernel, aways, first),
        out_shape=jax.ShapeDtypeStruct((PLANE, n * QBLK + 16, DH), BF),
        in_specs=[SMEM, ANY, VMEM, VMEM],
        out_specs=VMEM,
        scratch_shapes=[
            pltpu.VMEM((PLANE, n * QBLK, DH), BF),
            pltpu.VMEM((slots, 1, DH), F32),
            pltpu.SMEM((slots + UNROLL,), jnp.int32),
            pltpu.SemaphoreType.DMA,
        ],
        compiler_params=params(),
        cost_estimate=pl.CostEstimate(
            flops=slots * 4 * QBLK * BLK * DH,
            bytes_accessed=12 * 2**20,
            transcendentals=slots * QBLK * BLK,
        ),
        name=f"far{n}",
    )(meta, tiles, past_key, past_value_t)


def own_kernel(aways, info_ref, kv_ref, *refs):
    n = len(aways)
    queries, out_ref, lse_ref = refs[:n], refs[n], refs[n + 1]
    z, column = info_ref[0], info_ref[1]
    half, part = z // 4, z % 4
    key_at = lax.broadcasted_iota(jnp.int32, (QBLK, QBLK), 0)
    row_at = lax.broadcasted_iota(jnp.int32, (QBLK, QBLK), 1)
    for j in range(n):
        group = (z + aways[j]) % NZ // 4

        @pl.loop(0, 4)
        def _(b):
            keys = kv_ref[b, group]
            values = kv_ref[b, 2 + group]
            block = (column - b + 4) % 4
            first = (block * 2 + half) * 4
            scores = [mxu(keys, queries[j][first + t]) for t in range(4)]
            scores = [
                jnp.where(key_at <= row_at + (t - part) * QBLK, s, NONE)
                for t, s in enumerate(scores)
            ]
            tops = [jnp.max(s, axis=0, keepdims=True) for s in scores]
            terms = [jnp.exp2((s - m) * EXP_SCALE) for s, m in zip(scores, tops)]
            totals = [jnp.sum(t, axis=0, keepdims=True) for t in terms]
            outs = [mxu(values, t.astype(BF)) for t in terms]
            sums = []
            for t in range(4):
                out_ref[j * 16 + block * 4 + t] = (outs[t] * (1.0 / totals[t])).astype(BF)
                x = tops[t] * EXP_SCALE + jnp.log2(totals[t])
                sums.append(x + jnp.where(part > t, NONE, 0.0))
            lse_ref[j * 4 + block] = jnp.concatenate(sums, axis=0)


def own(queries, aways, kv, info):
    n = len(queries)
    return pl.pallas_call(
        functools.partial(own_kernel, aways),
        out_shape=(
            jax.ShapeDtypeStruct((n * 16, DH, QBLK), BF),
            jax.ShapeDtypeStruct((n * 4, 4, QBLK), F32),
        ),
        in_specs=[SMEM] + [VMEM] * (n + 1),
        out_specs=(VMEM, VMEM),
        compiler_params=params(),
        cost_estimate=pl.CostEstimate(
            flops=n * 16 * 4 * QBLK * QBLK * DH,
            bytes_accessed=2 * n * 2**20,
            transcendentals=n * 16 * QBLK * QBLK,
        ),
        name=f"own{n}",
    )(info, kv, *queries)


def split3(x):
    high = x.astype(BF).astype(F32)
    mid = (x - high).astype(BF).astype(F32)
    return [high, mid, x - high - mid]


def merge_kernel(
    j, away, arrivals, spans, info_ref, table_ref, back_ref, own_ref, own_lse_ref, *refs
):
    half = info_ref[0] // 4
    arrived, outs = refs[: len(arrivals)], refs[len(arrivals) : -2]
    arrived_lse, new_lse = refs[-2:]
    tail_at = back_ref.shape[1] - 16
    for a, (low, count) in enumerate(arrivals):
        rows = arrived[a][count * 4].astype(F32)
        rows = rows[0:32] + rows[32:64] + rows[64:96]
        for b in range(count):
            arrived_lse[a, b] = rows[4 * b : 4 * b + 4]

    def four_tiles(b, out_ref, start):
        own_at = j * 4 + b // 2
        own_sums = own_lse_ref[own_at] + jnp.where(b % 2 == half, 0.0, NONE)
        coming = []
        for a, (low, count) in enumerate(arrivals):
            here = b - low
            inside = jnp.logical_and(here >= 0, here < count)
            here = jnp.clip(here, 0, count - 1)
            coming.append(
                (arrived[a], here, arrived_lse[a, here] + jnp.where(inside, 0.0, NONE))
            )
        sums_out = []
        for t in range(4):
            tile = b * 4 + t
            parts = [own_ref[own_at * 4 + t]]
            sums = [own_sums[t : t + 1]]
            for acc_ref, here, arrived_sums in coming:
                parts.append(acc_ref[here * 4 + t])
                sums.append(arrived_sums[t : t + 1])
            for k in range(TOPK):
                owner = table_ref[away * 128 + tile * TOPK + k]
                at = jnp.maximum(owner, 0)
                parts.append(back_ref[at, j * QBLK : (j + 1) * QBLK, :])
                tail = back_ref[at, tail_at:, :].astype(F32)
                x = tail[3 * j : 3 * j + 1] + tail[3 * j + 1 : 3 * j + 2]
                x = x + tail[3 * j + 2 : 3 * j + 3]
                sums.append(x + jnp.where(owner >= 0, 0.0, NONE))
            top = functools.reduce(jnp.maximum, sums)
            weights = [jnp.exp2(x - top) for x in sums]
            total = sum(weights)
            inverse = 1.0 / total
            value = sum(
                part.astype(F32) * (weight * inverse) for part, weight in zip(parts, weights)
            )
            if spans is None:
                rows = pl.multiple_of(tile * QBLK, QBLK)
                out_ref[pl.ds(rows, QBLK), :] = value.T.astype(BF)
            else:
                out_ref[tile - start * 4] = value.astype(BF)
                sums_out.append(top + jnp.log2(total))
        if spans is not None:
            new_lse[b] = jnp.concatenate(sums_out, axis=0)

    for out_ref, (start, stop) in zip(outs, spans or ((0, TILES // 4),)):
        pl.loop(start, stop)(functools.partial(four_tiles, out_ref=out_ref, start=start))
        if spans is not None:
            rows = [new_lse[b] for b in range(start, stop)]
            if stop - start < TILES // 4:
                rows.append(jnp.zeros((TILES - 4 * (stop - start), DH), F32))
            rows = split3(jnp.concatenate(rows, axis=0))
            rows.append(jnp.zeros((128 - 3 * TILES, DH), F32))
            out_ref[(stop - start) * 4] = jnp.concatenate(rows, axis=0).astype(BF)


def merge(j, away, info, table, back, own_part, arrivals, spans):
    places = tuple((low, (acc.shape[0] - 1) // 4) for low, acc in arrivals)
    if spans is None:
        out_shape = (jax.ShapeDtypeStruct((TILES * QBLK, DH), BF),)
    else:
        out_shape = tuple(
            jax.ShapeDtypeStruct(((stop - start) * 4 + 1, DH, QBLK), BF) for start, stop in spans
        )
    return pl.pallas_call(
        functools.partial(merge_kernel, j, away, places, spans),
        out_shape=out_shape,
        in_specs=[SMEM, SMEM] + [VMEM] * (3 + len(arrivals)),
        out_specs=(VMEM,) * len(out_shape),
        scratch_shapes=[
            pltpu.VMEM((max(1, len(arrivals)), TILES // 4, 4, QBLK), F32),
            pltpu.VMEM((TILES // 4, 4, QBLK), F32),
        ],
        compiler_params=params(),
        cost_estimate=pl.CostEstimate(
            flops=TILES * 12 * QBLK * DH, bytes_accessed=4 * 2**20, transcendentals=0
        ),
        name=f"merge{j}",
    )(info, table, back, *own_part, *[acc for _, acc in arrivals])


def ring(x, step, axis="z", size=NZ):
    return lax.ppermute(x, axis, [(i, (i + step) % size) for i in range(size)])


def after(x, *others):
    return lax.optimization_barrier((x,) + others)[0]


CHUNKS = ((0,), (1, 7), (2, 6), (3, 5), (4,))


def shards(queries, win_key, win_value, past_key, past_value, chosen):
    x, z = lax.axis_index("x"), lax.axis_index("z")

    with jax.named_scope("prepare"):
        tiles = queries.reshape(TILES, QBLK, DH).swapaxes(1, 2)
        mine = jnp.pad(chosen.reshape(1, REQ), ((0, 0), (0, 128 - REQ)), constant_values=-4)

    with jax.named_scope("column"):
        away = (z + jnp.arange(NZ, dtype=jnp.int32)) % NZ
        column = lax.all_to_all(jnp.broadcast_to(mine, (NZ, 128)), "z", 0, 0, tiled=True)
    right = left = tiles
    sources = [(tiles,)]
    for step in range(1, 4):
        with jax.named_scope(f"ring{step}"):
            right, left = ring(right, 1), ring(left, -1)
        sources.append((left, right))
    with jax.named_scope("ring4"):
        sources.append((jnp.concatenate([ring(right[:16], 1), ring(left[16:], -1)], axis=0),))

    def coded(lists):
        plane_ids = jnp.arange(PLANE, dtype=jnp.int32)
        owner_ids = (plane_ids // 4) * 32 + (plane_ids % 4) * 8 + z
        entry = jnp.arange(128, dtype=jnp.int32) // TOPK * 4 + lists % 4 + 1
        found = jnp.where((lists // 4)[None] == owner_ids[:, None, None], entry[None], 0)
        return jnp.sum(found, axis=2)

    def tiles_in(code):
        return (jnp.maximum(code - 1, 0) // 4).reshape(-1)

    with jax.named_scope("lists"):
        tile_of_mine = tiles_in(coded(mine))
        column = jnp.take(column, away, axis=0)
        owner = column // 4
        code = coded(column)
        group = 2 * x + away // 4
        meta = jnp.where(code > 0, (code - 1) % 4 * 8 + group[None], -1)
        meta = jnp.pad(meta, ((0, 0), (0, 128 - NZ)))
        tile_of = tiles_in(code)
        place = (owner // 32) * 4 + owner % 32 // 8
        table = jnp.where(jnp.logical_and(owner % 8 == z, owner >= 0), place, -1).reshape(-1)
        info = jnp.where(jnp.arange(128, dtype=jnp.int32) == 0, z, x)
        meta, table, tile_of, info = lax.optimization_barrier((meta, table, tile_of, info))

    with jax.named_scope("kv"):
        own_k = win_key.reshape(QBLK, 4, 2, DH).transpose(1, 2, 0, 3)
        own_v = win_value.reshape(QBLK, 4, 2, DH).transpose(1, 2, 3, 0)
        pieces = jnp.concatenate([own_k, own_v], axis=1)
        kv = [lax.dynamic_index_in_dim(pieces, x, axis=0, keepdims=False)]
        for d in range(1, 4):
            piece = lax.dynamic_index_in_dim(pieces, (x + d) % 4, axis=0, keepdims=False)
            kv.append(ring(piece, d, "x", 4))
        kv = jnp.stack(kv)
        past_value_t = past_value.T

    previous = []

    def exchange(send, *others):
        send = after(send, *previous, *others)
        got = lax.all_to_all(send, ("y", "c", "x"), 0, 0, tiled=True)
        previous[:] = [got]
        return got

    def forward(chunks, *others):
        refs = [t for c in chunks for t in sources[c]]
        aways = [d for c in chunks for d in CHUNKS[c]]
        return exchange(pack(refs, aways, tile_of), *others)

    def partial(c, got, first=0):
        with jax.named_scope(f"far{c}"):
            return far(got, first, CHUNKS[c], meta, past_key, past_value_t)

    def own_part(c):
        with jax.named_scope(f"own{c}"):
            return tuple(own(sources[c], CHUNKS[c], kv, info))

    def merged(c, back, arrivals):
        out = {}
        with jax.named_scope(f"merge{c}"):
            for low in (0, 4):
                for j, away_by in enumerate(CHUNKS[c]):
                    coming = arrivals.get((j, low), [])
                    coming = [(low, acc) for acc in coming]
                    span = ((low, low + 4),)
                    (out[j, low],) = merge(
                        j, away_by, info, table, back, owns[c], coming, span
                    )
        return out

    def onward(c, parts):
        with jax.named_scope(f"return{c}"):
            return {(j, low): [ring(acc, 1 - 2 * j)] for (j, low), acc in parts.items()}

    def arrived(arrivals):
        return [acc for (acc,) in arrivals.values()]

    with jax.named_scope("forward"):
        got0 = exchange(pack(sources[0], (0,), tile_of_mine), column, *sources[1])
        own0, own1 = own_part(0), own_part(1)
        meta = exchange(meta, past_value_t, *own0, *own1)[:, :NZ].reshape(-1)
        got12 = forward((1, 2))
        part0, own2 = partial(0, got0), own_part(2)
        got34 = forward((3, 4), part0, *own2)
        part2, own3, own4 = partial(2, got12, 2), own_part(3), own_part(4)
        part4 = partial(4, after(got34, part2, *own3, *own4), 2)
        part3, part1 = partial(3, got34), partial(1, got12)
    owns = [own0, own1, own2, own3, own4]
    with jax.named_scope("back"):
        back4 = exchange(part4)
        back3 = exchange(part3)
        parts = merged(4, back4, {})
        arrivals = onward(4, {(0, 0): parts[0, 0], (1, 4): parts[0, 4]})
        back2 = exchange(part2, part1, *arrived(arrivals))
        arrivals = onward(3, merged(3, back3, arrivals))
        back1 = exchange(part1, *arrived(arrivals))
        arrivals = onward(2, merged(2, back2, arrivals))
        back0 = exchange(part0, *arrived(arrivals))
        arrivals = onward(1, merged(1, back1, arrivals))
        arrivals = [(low, acc) for (_, low), (acc,) in arrivals.items()]
        return merge(0, 0, info, table, back0, own0, arrivals, None)[0]


def solution(mesh):
    inner = Mesh(mesh.devices.reshape(4, 2, 4, 8), ("y", "c", "x", "z"))
    rows, heads = ("y", "c"), ("x", "z")
    return jax.shard_map(
        shards,
        mesh=inner,
        in_specs=(
            P(rows, heads),
            P(rows + heads, None),
            P(rows + heads, None),
            P(rows + heads, None),
            P(rows + heads, None),
            P(rows, heads, None),
        ),
        out_specs=P(rows, heads),
        check_vma=False,
    )
```

time: 1020 us -> 384 us (0.38)
  waiting for transfers between devices: 534 us -> 118 us
  local copies, waits for them, and re-layouts: 203 us -> 54.5 us
  matrix products: 137 us -> 0 us
  Pallas kernels: 0 us -> 93.6 us
  starting transfers between devices: 78.7 us -> 113 us
  blocking collectives: 27.6 us -> 0 us
  other arithmetic: 28.4 us -> 2.28 us
    all_to_all x10, waiting for transfers between devices: 534 us -> 37 us  [the longest x9 34.9 us: exchange(): got = lax.all_to_all(send, ('y', 'c', 'x'), 0, 0, tiled=True)]
    dot_general x48 -> x0, matrix products: 137 us -> none  [the longest x16 65.6 us: far_slots(): jnp.einsum('gqt,gtd->gqd', softmax_terms.astype(jnp.bfloat16), value_tile...]
    gather x38 -> x1, local copies, waits for them, and re-layouts: 112 us -> 0.55 us  [shards(): column = jnp.take(column, away, axis=0)]
    pallas_call x0 -> x28, Pallas kernels: none -> 93.6 us  [the longest x5 42.6 us: far(): pl.pallas_call(functools.partial(far_kernel, aways, first), out_shape=jax...]
    ppermute x0 -> x25, waiting for transfers between devices: none -> 81.3 us  [ring(): return lax.ppermute(x, axis, [(i, (i + step) % size) for i in range(size)])]
    all_to_all x8 -> x0, local copies, waits for them, and re-layouts: 42.8 us -> none  [the longest x1 10.3 us: shards(): lax.all_to_all(lax.all_to_all(send_tiles, 'ctx', split_axis=0, concat_axi...]
    unnamed x15 -> x121, local copies, waits for them, and re-layouts: 5.53 us -> 47.5 us
    ppermute x0 -> x25, starting transfers between devices: none -> 37.4 us  [ring(): return lax.ppermute(x, axis, [(i, (i + step) % size) for i in range(size)])]
  transfers between devices with their start and end apart: 10 -> 35, of which waited for: 6 -> 15; matrix products, arithmetic and copies ran while one was open for 34% -> 4% of each run, Pallas kernels for 0% -> 21%
where the time goes in v1:
time: 384 us; the launch traced here: 383 us
  waiting for transfers between devices  118 us (31%)
  starting transfers between devices  113 us (29%)
  Pallas kernels  93.6 us (24%)
  local copies, waits for them, and re-layouts  54.5 us (14%)
    ppermute x25, waiting for transfers between devices, ring(): return lax.ppermute(x, axis, [(i, (i + step) % size) for i in range(size)])  81.3 us
    all_to_all x9, starting transfers between devices, exchange(): got = lax.all_to_all(send, ('y', 'c', 'x'), 0, 0, tiled=True)  70.7 us
    unnamed x121, local copies, waits for them, and re-layouts  47.5 us
    pallas_call x5, Pallas kernels, far(): pl.pallas_call(functools.partial(far_kernel, aways, first), out_shape=jax...  42.6 us
    ppermute x25, starting transfers between devices, ring(): return lax.ppermute(x, axis, [(i, (i + step) % size) for i in range(size)])  37.4 us
    all_to_all x9, waiting for transfers between devices, exchange(): got = lax.all_to_all(send, ('y', 'c', 'x'), 0, 0, tiled=True)  34.9 us
    pallas_call x15, Pallas kernels, merge(): pl.pallas_call(functools.partial(merge_kernel, j, away, places, spans), o...  25.8 us
    pallas_call x5, Pallas kernels, own(): pl.pallas_call(functools.partial(own_kernel, aways), out_shape=(jax.Shape...  16.9 us
  transfers between devices with their start and end apart: 35, of which 15 were waited for; matrix products, arithmetic and copies ran while one was open for 4% of the time, Pallas kernels for 21%

profile of v1, /device:TPU:1, one launch (start us, length us, event | category | flops | bytes accessed | tf_op | source)
XLA Modules:
  0.0 382.7 jit_solution(315259654466977530)
XLA Ops:
  4.2 4.0 %collective-permute-start = (bf16[32,128,128]{2,1,0:T(8,128)(2,1)S(1)}, bf16[32,128,128]{2,1,0:T(8,128)(2,1)}, u32[]{:S(2)}, u32[]{:S(2)}) collective-permute-start(bf16[32,128,128]{2,1,0:T(8,128)(2,1)S(1)} %bitcast.52), channel_id=1, source_target_pairs={{0,7},{1,0},{2,1},{3,2},{4,3},{5,4},{6,5},{7,6},{8,15},{9,8},{10,9... | collective-permute-start | bytes 3145736 | tf_op jit(solution)/shard_map/ring1/ppermute | solution.py:305
  9.7 5.2 %all-to-all-start = ((s32[8,1,128]{2,1,0:T(1,128)}), s32[8,1,128]{2,1,0:T(1,128)S(1)}, u32[]{:S(2)}, u32[]{:S(2)}) async-start(s32[8,1,128]{2,1,0:T(1,128)} %broadcast_in_dim.61), calls=%async_computation | async-start | bytes 8192 | tf_op jit(solution)/shard_map/column/all_to_all | solution.py:324
  23.9 6.5 %copy.24 = bf16[2048,1024]{0,1:T(8,128)(2,1)} copy(bf16[2048,1024]{1,0:T(8,128)(2,1)} %param.10) | data formatting | bytes 8388608 | tf_op args[4]
  33.9 9.0 %all-to-all-start.1 = ((bf16[32,128,128]{2,1,0:T(8,128)(2,1)}), bf16[32,128,128]{2,1,0:T(8,128)(2,1)}, u32[]{:S(2)}, u32[]{:S(2)}) async-start(bf16[32,128,128]{2,1,0:T(8,128)(2,1)} %copy-done.23), calls=%async_computation.1 | async-start | bytes 2097152 | tf_op jit(solution)/shard_map/forward/all_to_all | solution.py:373
  51.3 4.3 %own2.3 = (bf16[32,128,128]{2,1,0:T(8,128)(2,1)S(1)}, f32[8,4,128]{2,1,0:T(4,128)S(1)}) custom-call(s32[128]{0:T(128)S(1)} %compare_select_fusion.5.info_ref, bf16[4,4,128,128]{3,2,1,0:T(8,128)(2,1)S(1)} %pad_maximum_fusion.kv_ref, bf16[32,128,128]{2,1,0:T(8,128)(2,1)} %collective-permute-done.refs_0_, bf16[32,128,128]{2,1,0:T(8,128)(2,1)S(1)} %collective-permute-done.1.refs_1_), custom_call_target="tpu_custom_call" | custom-call | flops 268435456 | bytes 4194304 | tf_op jit(solution)/shard_map/forward/own1/own2/pallas_call | solution.py:188
  58.9 5.6 %all-to-all-start.2 = ((s32[32,1,128]{2,1,0:T(1,128)}), s32[32,1,128]{2,1,0:T(1,128)S(1)}, u32[]{:S(2)}, u32[]{:S(2)}) async-start(s32[32,1,128]{2,1,0:T(1,128)} %bitcast.20), calls=%async_computation.2 | async-start | bytes 32768 | tf_op jit(solution)/shard_map/forward/all_to_all | solution.py:373
  64.6 4.2 %collective-permute-done.6.refs_3_.refs_1_ = bf16[32,128,128]{2,1,0:T(8,128)(2,1)} collective-permute-done((bf16[32,128,128]{2,1,0:T(8,128)(2,1)S(1)}, bf16[32,128,128]{2,1,0:T(8,128)(2,1)}, u32[]{:S(2)}, u32[]{:S(2)}) %collective-permute-start.6) | collective-permute-done | bytes 1048608 | tf_op jit(solution)/shard_map/ring2/ppermute | solution.py:305
  69.6 3.9 %pack4.1 = bf16[32,512,128]{2,1,0:T(8,128)(2,1)} custom-call(s32[256]{0:T(256)S(1)} %add_select_fusion.8.idx_ref, bf16[32,128,128]{2,1,0:T(8,128)(2,1)} %collective-permute-done.refs_0_, bf16[32,128,128]{2,1,0:T(8,128)(2,1)S(1)} %collective-permute-done.1.refs_1_, bf16[32,128,128]{2,1,0:T(8,128)(2,1)} %collective-permute-done.5.refs_2_.refs_0_, ...), custom_call_target="tpu_custom_call" | custom-call | bytes 8388608 | tf_op jit(solution)/shard_map/forward/pack4/pallas_call | solution.py:57
  73.6 8.5 %all-to-all-start.3 = ((bf16[32,512,128]{2,1,0:T(8,128)(2,1)}), bf16[32,512,128]{2,1,0:T(8,128)(2,1)}, u32[]{:S(2)}, u32[]{:S(2)}) async-start(bf16[32,512,128]{2,1,0:T(8,128)(2,1)} %pack4.1), calls=%async_computation.3 | async-start | bytes 8388608 | tf_op jit(solution)/shard_map/forward/all_to_all | solution.py:373
  84.9 23.3 %collective-permute-done.8.refs_1_ = bf16[32,128,128]{2,1,0:T(8,128)(2,1)S(1)} collective-permute-done((bf16[32,128,128]{2,1,0:T(8,128)(2,1)}, bf16[32,128,128]{2,1,0:T(8,128)(2,1)S(1)}, u32[]{:S(2)}, u32[]{:S(2)}) %collective-permute-start.8) | collective-permute-done | bytes 1048608 | tf_op jit(solution)/shard_map/ring3/ppermute | solution.py:305
  112.8 6.4 %far1.2 = bf16[32,144,128]{2,1,0:T(8,128)(2,1)S(1)} custom-call(s32[256]{0:T(256)S(1)} %reshape.340.meta_ref, bf16[32,128,128]{2,1,0:T(8,128)(2,1)} %all-to-all-done.1.got_ref, bf16[2048,1024]{1,0:T(8,128)(2,1)} %k_ref.9, bf16[1024,2048]{1,0:T(8,128)(2,1)} %bitcast.55), custom_call_target="tpu_custom_call" | custom-call | flops 1073741824 | bytes 12582912 | tf_op jit(solution)/shard_map/forward/far0/far1/pallas_call | solution.py:132
  120.3 4.7 %own2.4 = (bf16[32,128,128]{2,1,0:T(8,128)(2,1)S(1)}, f32[8,4,128]{2,1,0:T(4,128)S(1)}) custom-call(s32[128]{0:T(128)S(1)} %compare_select_fusion.5.info_ref, bf16[4,4,128,128]{3,2,1,0:T(8,128)(2,1)S(1)} %pad_maximum_fusion.kv_ref, bf16[32,128,128]{2,1,0:T(8,128)(2,1)} %collective-permute-done.5.refs_2_.refs_0_, ...), custom_call_target="tpu_custom_call" | custom-call | flops 268435456 | bytes 4194304 | tf_op jit(solution)/shard_map/forward/own2/own2/pallas_call | solution.py:188
  131.7 9.5 %all-to-all-start.4 = ((bf16[32,384,128]{2,1,0:T(8,128)(2,1)}), bf16[32,384,128]{2,1,0:T(8,128)(2,1)S(1)}, u32[]{:S(2)}, u32[]{:S(2)}) async-start(bf16[32,384,128]{2,1,0:T(8,128)(2,1)} %pack3.1), calls=%async_computation.4 | async-start | bytes 6291456 | tf_op jit(solution)/shard_map/forward/all_to_all | solution.py:373
  151.3 10.5 %far2.4 = bf16[32,272,128]{2,1,0:T(8,128)(2,1)S(1)} custom-call(s32[256]{0:T(256)S(1)} %reshape.340.meta_ref, bf16[32,512,128]{2,1,0:T(8,128)(2,1)} %all-to-all-done.3.got_ref, bf16[2048,1024]{1,0:T(8,128)(2,1)} %k_ref.9, bf16[1024,2048]{1,0:T(8,128)(2,1)} %bitcast.56), custom_call_target="tpu_custom_call" | custom-call | flops 2147483648 | bytes 12582912 | tf_op jit(solution)/shard_map/forward/far2/far2/pallas_call | solution.py:132
  163.2 16.0 %all-to-all-done.4.got_ref = bf16[32,384,128]{2,1,0:T(8,128)(2,1)S(1)} async-done(((bf16[32,384,128]{2,1,0:T(8,128)(2,1)}), bf16[32,384,128]{2,1,0:T(8,128)(2,1)S(1)}, u32[]{:S(2)}, u32[]{:S(2)}) %all-to-all-start.4) | async-done | bytes 3145760 | tf_op jit(solution)/shard_map/forward/all_to_all | solution.py:373
  179.2 6.4 %far1.3 = bf16[32,144,128]{2,1,0:T(8,128)(2,1)S(1)} custom-call(s32[256]{0:T(256)S(1)} %reshape.340.meta_ref, bf16[32,384,128]{2,1,0:T(8,128)(2,1)S(1)} %all-to-all-done.4.got_ref, bf16[2048,1024]{1,0:T(8,128)(2,1)} %k_ref.9, bf16[1024,2048]{1,0:T(8,128)(2,1)} %bitcast.57), custom_call_target="tpu_custom_call" | custom-call | flops 1073741824 | bytes 12582912 | tf_op jit(solution)/shard_map/forward/far4/far1/pallas_call | solution.py:132
  186.6 8.9 %all-to-all-start.5 = ((bf16[32,144,128]{2,1,0:T(8,128)(2,1)}), bf16[32,144,128]{2,1,0:T(8,128)(2,1)}, u32[]{:S(2)}, u32[]{:S(2)}) async-start(bf16[32,144,128]{2,1,0:T(8,128)(2,1)} %copy-done.21), calls=%async_computation.5 | async-start | bytes 2359296 | tf_op jit(solution)/shard_map/back/all_to_all | solution.py:373
  195.5 9.4 %far2.5 = bf16[32,272,128]{2,1,0:T(8,128)(2,1)S(1)} custom-call(s32[256]{0:T(256)S(1)} %reshape.340.meta_ref, bf16[32,384,128]{2,1,0:T(8,128)(2,1)S(1)} %all-to-all-done.4.got_ref, bf16[2048,1024]{1,0:T(8,128)(2,1)} %k_ref.9, bf16[1024,2048]{1,0:T(8,128)(2,1)} %bitcast.58), custom_call_target="tpu_custom_call" | custom-call | flops 2147483648 | bytes 12582912 | tf_op jit(solution)/shard_map/forward/far3/far2/pallas_call | solution.py:132
  206.3 6.6 %all-to-all-done.5.back_ref = bf16[32,144,128]{2,1,0:T(8,128)(2,1)} async-done(((bf16[32,144,128]{2,1,0:T(8,128)(2,1)}), bf16[32,144,128]{2,1,0:T(8,128)(2,1)}, u32[]{:S(2)}, u32[]{:S(2)}) %all-to-all-start.5) | async-done | bytes 1179680 | tf_op jit(solution)/shard_map/back/all_to_all | solution.py:373
  212.9 7.2 %all-to-all-start.6 = ((bf16[32,272,128]{2,1,0:T(8,128)(2,1)}), bf16[32,272,128]{2,1,0:T(8,128)(2,1)S(1)}, u32[]{:S(2)}, u32[]{:S(2)}) async-start(bf16[32,272,128]{2,1,0:T(8,128)(2,1)} %copy-done.12), calls=%async_computation.6 | async-start | bytes 4456448 | tf_op jit(solution)/shard_map/back/all_to_all | solution.py:373
  226.9 9.9 %far2.3 = bf16[32,272,128]{2,1,0:T(8,128)(2,1)S(1)} custom-call(s32[256]{0:T(256)S(1)} %reshape.340.meta_ref, bf16[32,512,128]{2,1,0:T(8,128)(2,1)} %all-to-all-done.3.got_ref, bf16[2048,1024]{1,0:T(8,128)(2,1)} %k_ref.9, bf16[1024,2048]{1,0:T(8,128)(2,1)} %bitcast.59), custom_call_target="tpu_custom_call" | custom-call | flops 2147483648 | bytes 12582912 | tf_op jit(solution)/shard_map/forward/far1/far2/pallas_call | solution.py:132
  239.8 8.6 %all-to-all-done.6.back_ref = bf16[32,272,128]{2,1,0:T(8,128)(2,1)S(1)} async-done(((bf16[32,272,128]{2,1,0:T(8,128)(2,1)}), bf16[32,272,128]{2,1,0:T(8,128)(2,1)S(1)}, u32[]{:S(2)}, u32[]{:S(2)}) %all-to-all-start.6) | async-done | bytes 2228256 | tf_op jit(solution)/shard_map/back/all_to_all | solution.py:373
  249.7 5.5 %all-to-all-start.7 = ((bf16[32,272,128]{2,1,0:T(8,128)(2,1)}), bf16[32,272,128]{2,1,0:T(8,128)(2,1)S(1)}, u32[]{:S(2)}, u32[]{:S(2)}) async-start(bf16[32,272,128]{2,1,0:T(8,128)(2,1)} %copy-done.14), calls=%async_computation.7 | async-start | bytes 4456448 | tf_op jit(solution)/shard_map/back/all_to_all | solution.py:373
  268.0 6.6 %collective-permute-done.13.refs_0_ = bf16[17,128,128]{2,1,0:T(8,128)(2,1)S(1)} collective-permute-done((bf16[17,128,128]{2,1,0:T(8,128)(2,1)S(1)}, bf16[17,128,128]{2,1,0:T(8,128)(2,1)S(1)}, u32[]{:S(2)}, u32[]{:S(2)}) %collective-permute-start.13) | collective-permute-done | bytes 557088 | tf_op jit(solution)/shard_map/back/return3/ppermute | solution.py:305
  276.3 11.1 %collective-permute-done.14.refs_0_ = bf16[17,128,128]{2,1,0:T(8,128)(2,1)S(1)} collective-permute-done((bf16[17,128,128]{2,1,0:T(8,128)(2,1)S(1)}, bf16[17,128,128]{2,1,0:T(8,128)(2,1)S(1)}, u32[]{:S(2)}, u32[]{:S(2)}) %collective-permute-start.14) | collective-permute-done | bytes 557088 | tf_op jit(solution)/shard_map/back/return3/ppermute | solution.py:305
  290.4 8.4 %all-to-all-start.8 = ((bf16[32,272,128]{2,1,0:T(8,128)(2,1)}), bf16[32,272,128]{2,1,0:T(8,128)(2,1)S(1)}, u32[]{:S(2)}, u32[]{:S(2)}) async-start(bf16[32,272,128]{2,1,0:T(8,128)(2,1)} %copy-done.13), calls=%async_computation.8 | async-start | bytes 4456448 | tf_op jit(solution)/shard_map/back/all_to_all | solution.py:373
  312.3 6.8 %collective-permute-done.17.refs_0_ = bf16[17,128,128]{2,1,0:T(8,128)(2,1)S(1)} collective-permute-done((bf16[17,128,128]{2,1,0:T(8,128)(2,1)S(1)}, bf16[17,128,128]{2,1,0:T(8,128)(2,1)S(1)}, u32[]{:S(2)}, u32[]{:S(2)}) %collective-permute-start.17) | collective-permute-done | bytes 557088 | tf_op jit(solution)/shard_map/back/return2/ppermute | solution.py:305
  320.7 10.8 %collective-permute-done.18.refs_0_ = bf16[17,128,128]{2,1,0:T(8,128)(2,1)S(1)} collective-permute-done((bf16[17,128,128]{2,1,0:T(8,128)(2,1)S(1)}, bf16[17,128,128]{2,1,0:T(8,128)(2,1)S(1)}, u32[]{:S(2)}, u32[]{:S(2)}) %collective-permute-start.18) | collective-permute-done | bytes 557088 | tf_op jit(solution)/shard_map/back/return2/ppermute | solution.py:305
  333.2 8.1 %all-to-all-start.9 = ((bf16[32,144,128]{2,1,0:T(8,128)(2,1)}), bf16[32,144,128]{2,1,0:T(8,128)(2,1)}, u32[]{:S(2)}, u32[]{:S(2)}) async-start(bf16[32,144,128]{2,1,0:T(8,128)(2,1)} %copy-done.22), calls=%async_computation.9 | async-start | bytes 2359296 | tf_op jit(solution)/shard_map/back/all_to_all | solution.py:373
  353.3 6.8 %collective-permute-done.21.refs_0_ = bf16[17,128,128]{2,1,0:T(8,128)(2,1)S(1)} collective-permute-done((bf16[17,128,128]{2,1,0:T(8,128)(2,1)S(1)}, bf16[17,128,128]{2,1,0:T(8,128)(2,1)S(1)}, u32[]{:S(2)}, u32[]{:S(2)}) %collective-permute-start.21) | collective-permute-done | bytes 557088 | tf_op jit(solution)/shard_map/back/return1/ppermute | solution.py:305
  361.7 10.8 %collective-permute-done.24.refs_3_ = bf16[17,128,128]{2,1,0:T(8,128)(2,1)S(1)} collective-permute-done((bf16[17,128,128]{2,1,0:T(8,128)(2,1)S(1)}, bf16[17,128,128]{2,1,0:T(8,128)(2,1)S(1)}, u32[]{:S(2)}, u32[]{:S(2)}) %collective-permute-start.24) | collective-permute-done | bytes 557088 | tf_op jit(solution)/shard_map/back/return1/ppermute | solution.py:305
  377.6 5.1 %merge0.17 = bf16[4096,128]{1,0:T(8,128)(2,1)} custom-call(s32[128]{0:T(128)S(1)} %compare_select_fusion.5.info_ref, s32[1024]{0:T(1024)S(1)} %fusion.18.table_ref, bf16[32,144,128]{2,1,0:T(8,128)(2,1)} %all-to-all-done.9.back_ref, bf16[16,128,128]{2,1,0:T(8,128)(2,1)S(1)} %copy-done.53, f32[4,4,128]{2,1,0:T(4,128)S(1)} %get-tuple-element.34.own_lse_ref, ...), custom_call_target="tpu_custom_call" | custom-call | flops 6291456 | bytes 4194304 | tf_op jit(solution)/shard_map/back/merge0/pallas_call | solution.py:287
  (218 shorter events, 123.3 us)
Async XLA Ops:
  1.7 32.2 %collective-permute-start.1 = (bf16[32,128,128]{2,1,0:T(8,128)(2,1)S(1)}, bf16[32,128,128]{2,1,0:T(8,128)(2,1)S(1)}, u32[]{:S(2)}, u32[]{:S(2)}) collective-permute-start(bf16[32,128,128]{2,1,0:T(8,128)(2,1)S(1)} %bitcast.51), channel_id=1, source_target_pairs={{0,1},{1,2},{2,3},{3,4},{4,5},{5,6},{6,7},{7,0},{8,9},{9,10},{10,1... | collective-permute-start | bytes 3145736 | tf_op jit(solution)/shard_map/ring1/ppermute | solution.py:305
  4.2 29.6 %collective-permute-start = (bf16[32,128,128]{2,1,0:T(8,128)(2,1)S(1)}, bf16[32,128,128]{2,1,0:T(8,128)(2,1)}, u32[]{:S(2)}, u32[]{:S(2)}) collective-permute-start(bf16[32,128,128]{2,1,0:T(8,128)(2,1)S(1)} %bitcast.52), channel_id=1, source_target_pairs={{0,7},{1,0},{2,1},{3,2},{4,3},{5,4},{6,5},{7,6},{8,15},{9,8},{10,9... | collective-permute-start | bytes 3145736 | tf_op jit(solution)/shard_map/ring1/ppermute | solution.py:305
  9.7 22.8 %all-to-all-start = ((s32[8,1,128]{2,1,0:T(1,128)}), s32[8,1,128]{2,1,0:T(1,128)S(1)}, u32[]{:S(2)}, u32[]{:S(2)}) async-start(s32[8,1,128]{2,1,0:T(1,128)} %broadcast_in_dim.61), calls=%async_computation | async-start | bytes 8192 | tf_op jit(solution)/shard_map/column/all_to_all | solution.py:324
  15.6 31.0 %collective-permute-start.2 = (bf16[4,128,128]{2,1,0:T(8,128)(2,1)S(1)}, bf16[4,128,128]{2,1,0:T(8,128)(2,1)S(1)}, u32[]{:S(2)}, u32[]{:S(2)}) collective-permute-start(bf16[4,128,128]{2,1,0:T(8,128)(2,1)S(1)} %get-tuple-element.56), channel_id=1, source_target_pairs={{0,8},{8,16},{16,24},{24,0},{1,9},{9,17},{17,25},{25,1},{2,10},{10... | collective-permute-start | bytes 393224 | tf_op jit(solution)/shard_map/kv/ppermute | solution.py:305
  16.9 29.7 %collective-permute-start.3 = (bf16[4,128,128]{2,1,0:T(8,128)(2,1)S(1)}, bf16[4,128,128]{2,1,0:T(8,128)(2,1)S(1)}, u32[]{:S(2)}, u32[]{:S(2)}) collective-permute-start(bf16[4,128,128]{2,1,0:T(8,128)(2,1)S(1)} %get-tuple-element.57), channel_id=1, source_target_pairs={{0,16},{8,24},{16,0},{24,8},{1,17},{9,25},{17,1},{25,9},{2,18},{10... | collective-permute-start | bytes 393224 | tf_op jit(solution)/shard_map/kv/ppermute | solution.py:305
  19.3 27.3 %collective-permute-start.4 = (bf16[4,128,128]{2,1,0:T(8,128)(2,1)S(1)}, bf16[4,128,128]{2,1,0:T(8,128)(2,1)S(1)}, u32[]{:S(2)}, u32[]{:S(2)}) collective-permute-start(bf16[4,128,128]{2,1,0:T(8,128)(2,1)S(1)} %get-tuple-element.58), channel_id=1, source_target_pairs={{0,24},{8,0},{16,8},{24,16},{1,25},{9,1},{17,9},{25,17},{2,26},{10... | collective-permute-start | bytes 393224 | tf_op jit(solution)/shard_map/kv/ppermute | solution.py:305
  33.9 25.1 %all-to-all-start.1 = ((bf16[32,128,128]{2,1,0:T(8,128)(2,1)}), bf16[32,128,128]{2,1,0:T(8,128)(2,1)}, u32[]{:S(2)}, u32[]{:S(2)}) async-start(bf16[32,128,128]{2,1,0:T(8,128)(2,1)} %copy-done.23), calls=%async_computation.1 | async-start | bytes 2097152 | tf_op jit(solution)/shard_map/forward/all_to_all | solution.py:373
  42.9 25.8 %collective-permute-start.6 = (bf16[32,128,128]{2,1,0:T(8,128)(2,1)S(1)}, bf16[32,128,128]{2,1,0:T(8,128)(2,1)}, u32[]{:S(2)}, u32[]{:S(2)}) collective-permute-start(bf16[32,128,128]{2,1,0:T(8,128)(2,1)S(1)} %collective-permute-done.1.refs_1_), channel_id=1, source_target_pairs={{0,1},{1,2},{2,3},{3,4},{4,5},{5,6},{6,7},{7,0},{8,9},{9,10},{10,1... | collective-permute-start | bytes 3145736 | tf_op jit(solution)/shard_map/ring2/ppermute | solution.py:305
  45.2 24.4 %collective-permute-start.5 = (bf16[32,128,128]{2,1,0:T(8,128)(2,1)}, bf16[32,128,128]{2,1,0:T(8,128)(2,1)}, u32[]{:S(2)}, u32[]{:S(2)}) collective-permute-start(bf16[32,128,128]{2,1,0:T(8,128)(2,1)} %collective-permute-done.refs_0_), channel_id=1, source_target_pairs={{0,7},{1,0},{2,1},{3,2},{4,3},{5,4},{6,5},{7,6},{8,15},{9,8},{10,9... | collective-permute-start | bytes 3145736 | tf_op jit(solution)/shard_map/ring2/ppermute | solution.py:305
  73.6 58.1 %all-to-all-start.3 = ((bf16[32,512,128]{2,1,0:T(8,128)(2,1)}), bf16[32,512,128]{2,1,0:T(8,128)(2,1)}, u32[]{:S(2)}, u32[]{:S(2)}) async-start(bf16[32,512,128]{2,1,0:T(8,128)(2,1)} %pack4.1), calls=%async_computation.3 | async-start | bytes 8388608 | tf_op jit(solution)/shard_map/forward/all_to_all | solution.py:373
  82.1 26.0 %collective-permute-start.8 = (bf16[32,128,128]{2,1,0:T(8,128)(2,1)}, bf16[32,128,128]{2,1,0:T(8,128)(2,1)S(1)}, u32[]{:S(2)}, u32[]{:S(2)}) collective-permute-start(bf16[32,128,128]{2,1,0:T(8,128)(2,1)} %collective-permute-done.6.refs_3_.refs_1_), channel_id=1, source_target_pairs={{0,1},{1,2},{2,3},{3,4},{4,5},{5,6},{6,7},{7,0},{8,9},{9,10},{10,1... | collective-permute-start | bytes 3145736 | tf_op jit(solution)/shard_map/ring3/ppermute | solution.py:305
  82.5 26.6 %collective-permute-start.7 = (bf16[32,128,128]{2,1,0:T(8,128)(2,1)}, bf16[32,128,128]{2,1,0:T(8,128)(2,1)S(1)}, u32[]{:S(2)}, u32[]{:S(2)}) collective-permute-start(bf16[32,128,128]{2,1,0:T(8,128)(2,1)} %collective-permute-done.5.refs_2_.refs_0_), channel_id=1, source_target_pairs={{0,7},{1,0},{2,1},{3,2},{4,3},{5,4},{6,5},{7,6},{8,15},{9,8},{10,9... | collective-permute-start | bytes 3145736 | tf_op jit(solution)/shard_map/ring3/ppermute | solution.py:305
  109.1 16.9 %collective-permute-start.9 = (bf16[16,128,128]{2,1,0:T(8,128)(2,1)}, bf16[16,128,128]{2,1,0:T(8,128)(2,1)S(1)}, u32[]{:S(2)}, u32[]{:S(2)}) collective-permute-start(bf16[16,128,128]{2,1,0:T(8,128)(2,1)} %slice.15), channel_id=1, source_target_pairs={{0,1},{1,2},{2,3},{3,4},{4,5},{5,6},{6,7},{7,0},{8,9},{9,10},{10,1... | collective-permute-start | bytes 1572872 | tf_op jit(solution)/shard_map/ring4/ppermute | solution.py:305
  110.1 15.9 %collective-permute-start.10 = (bf16[16,128,128]{2,1,0:T(8,128)(2,1)}, bf16[16,128,128]{2,1,0:T(8,128)(2,1)}, u32[]{:S(2)}, u32[]{:S(2)}) collective-permute-start(bf16[16,128,128]{2,1,0:T(8,128)(2,1)} %slice.16), channel_id=1, source_target_pairs={{0,7},{1,0},{2,1},{3,2},{4,3},{5,4},{6,5},{7,6},{8,15},{9,8},{10,9... | collective-permute-start | bytes 1572872 | tf_op jit(solution)/shard_map/ring4/ppermute | solution.py:305
  131.7 47.5 %all-to-all-start.4 = ((bf16[32,384,128]{2,1,0:T(8,128)(2,1)}), bf16[32,384,128]{2,1,0:T(8,128)(2,1)S(1)}, u32[]{:S(2)}, u32[]{:S(2)}) async-start(bf16[32,384,128]{2,1,0:T(8,128)(2,1)} %pack3.1), calls=%async_computation.4 | async-start | bytes 6291456 | tf_op jit(solution)/shard_map/forward/all_to_all | solution.py:373
  186.6 26.3 %all-to-all-start.5 = ((bf16[32,144,128]{2,1,0:T(8,128)(2,1)}), bf16[32,144,128]{2,1,0:T(8,128)(2,1)}, u32[]{:S(2)}, u32[]{:S(2)}) async-start(bf16[32,144,128]{2,1,0:T(8,128)(2,1)} %copy-done.21), calls=%async_computation.5 | async-start | bytes 2359296 | tf_op jit(solution)/shard_map/back/all_to_all | solution.py:373
  212.9 35.4 %all-to-all-start.6 = ((bf16[32,272,128]{2,1,0:T(8,128)(2,1)}), bf16[32,272,128]{2,1,0:T(8,128)(2,1)S(1)}, u32[]{:S(2)}, u32[]{:S(2)}) async-start(bf16[32,272,128]{2,1,0:T(8,128)(2,1)} %copy-done.12), calls=%async_computation.6 | async-start | bytes 4456448 | tf_op jit(solution)/shard_map/back/all_to_all | solution.py:373
  222.1 16.0 %collective-permute-start.11 = (bf16[17,128,128]{2,1,0:T(8,128)(2,1)S(1)}, bf16[17,128,128]{2,1,0:T(8,128)(2,1)S(1)}, u32[]{:S(2)}, u32[]{:S(2)}) collective-permute-start(bf16[17,128,128]{2,1,0:T(8,128)(2,1)S(1)} %merge0.9), channel_id=1, source_target_pairs={{0,1},{1,2},{2,3},{3,4},{4,5},{5,6},{6,7},{7,0},{8,9},{9,10},{10,1... | collective-permute-start | bytes 1671176 | tf_op jit(solution)/shard_map/back/return4/ppermute | solution.py:305
  249.7 39.3 %all-to-all-start.7 = ((bf16[32,272,128]{2,1,0:T(8,128)(2,1)}), bf16[32,272,128]{2,1,0:T(8,128)(2,1)S(1)}, u32[]{:S(2)}, u32[]{:S(2)}) async-start(bf16[32,272,128]{2,1,0:T(8,128)(2,1)} %copy-done.14), calls=%async_computation.7 | async-start | bytes 4456448 | tf_op jit(solution)/shard_map/back/all_to_all | solution.py:373
  259.4 15.3 %collective-permute-start.13 = (bf16[17,128,128]{2,1,0:T(8,128)(2,1)S(1)}, bf16[17,128,128]{2,1,0:T(8,128)(2,1)S(1)}, u32[]{:S(2)}, u32[]{:S(2)}) collective-permute-start(bf16[17,128,128]{2,1,0:T(8,128)(2,1)S(1)} %merge0.11), channel_id=1, source_target_pairs={{0,1},{1,2},{2,3},{3,4},{4,5},{5,6},{6,7},{7,0},{8,9},{9,10},{10,1... | collective-permute-start | bytes 1671176 | tf_op jit(solution)/shard_map/back/return3/ppermute | solution.py:305
  265.1 22.3 %collective-permute-start.14 = (bf16[17,128,128]{2,1,0:T(8,128)(2,1)S(1)}, bf16[17,128,128]{2,1,0:T(8,128)(2,1)S(1)}, u32[]{:S(2)}, u32[]{:S(2)}) collective-permute-start(bf16[17,128,128]{2,1,0:T(8,128)(2,1)S(1)} %merge1.6), channel_id=1, source_target_pairs={{0,7},{1,0},{2,1},{3,2},{4,3},{5,4},{6,5},{7,6},{8,15},{9,8},{10,9... | collective-permute-start | bytes 1671176 | tf_op jit(solution)/shard_map/back/return3/ppermute | solution.py:305
  266.5 21.7 %collective-permute-start.15 = (bf16[17,128,128]{2,1,0:T(8,128)(2,1)S(1)}, bf16[17,128,128]{2,1,0:T(8,128)(2,1)S(1)}, u32[]{:S(2)}, u32[]{:S(2)}) collective-permute-start(bf16[17,128,128]{2,1,0:T(8,128)(2,1)S(1)} %merge0.12), channel_id=1, source_target_pairs={{0,1},{1,2},{2,3},{3,4},{4,5},{5,6},{6,7},{7,0},{8,9},{9,10},{10,1... | collective-permute-start | bytes 1671176 | tf_op jit(solution)/shard_map/back/return3/ppermute | solution.py:305
  290.4 42.8 %all-to-all-start.8 = ((bf16[32,272,128]{2,1,0:T(8,128)(2,1)}), bf16[32,272,128]{2,1,0:T(8,128)(2,1)S(1)}, u32[]{:S(2)}, u32[]{:S(2)}) async-start(bf16[32,272,128]{2,1,0:T(8,128)(2,1)} %copy-done.13), calls=%async_computation.8 | async-start | bytes 4456448 | tf_op jit(solution)/shard_map/back/all_to_all | solution.py:373
  303.0 16.2 %collective-permute-start.17 = (bf16[17,128,128]{2,1,0:T(8,128)(2,1)S(1)}, bf16[17,128,128]{2,1,0:T(8,128)(2,1)S(1)}, u32[]{:S(2)}, u32[]{:S(2)}) collective-permute-start(bf16[17,128,128]{2,1,0:T(8,128)(2,1)S(1)} %merge0.13), channel_id=1, source_target_pairs={{0,1},{1,2},{2,3},{3,4},{4,5},{5,6},{6,7},{7,0},{8,9},{9,10},{10,1... | collective-permute-start | bytes 1671176 | tf_op jit(solution)/shard_map/back/return2/ppermute | solution.py:305
  304.7 15.3 %collective-permute-start.20 = (bf16[17,128,128]{2,1,0:T(8,128)(2,1)S(1)}, bf16[17,128,128]{2,1,0:T(8,128)(2,1)S(1)}, u32[]{:S(2)}, u32[]{:S(2)}) collective-permute-start(bf16[17,128,128]{2,1,0:T(8,128)(2,1)S(1)} %merge1.9), channel_id=1, source_target_pairs={{0,7},{1,0},{2,1},{3,2},{4,3},{5,4},{6,5},{7,6},{8,15},{9,8},{10,9... | collective-permute-start | bytes 1671176 | tf_op jit(solution)/shard_map/back/return2/ppermute | solution.py:305
  309.3 22.3 %collective-permute-start.18 = (bf16[17,128,128]{2,1,0:T(8,128)(2,1)S(1)}, bf16[17,128,128]{2,1,0:T(8,128)(2,1)S(1)}, u32[]{:S(2)}, u32[]{:S(2)}) collective-permute-start(bf16[17,128,128]{2,1,0:T(8,128)(2,1)S(1)} %merge1.8), channel_id=1, source_target_pairs={{0,7},{1,0},{2,1},{3,2},{4,3},{5,4},{6,5},{7,6},{8,15},{9,8},{10,9... | collective-permute-start | bytes 1671176 | tf_op jit(solution)/shard_map/back/return2/ppermute | solution.py:305
  312.2 20.2 %collective-permute-start.19 = (bf16[17,128,128]{2,1,0:T(8,128)(2,1)S(1)}, bf16[17,128,128]{2,1,0:T(8,128)(2,1)S(1)}, u32[]{:S(2)}, u32[]{:S(2)}) collective-permute-start(bf16[17,128,128]{2,1,0:T(8,128)(2,1)S(1)} %merge0.14), channel_id=1, source_target_pairs={{0,1},{1,2},{2,3},{3,4},{4,5},{5,6},{6,7},{7,0},{8,9},{9,10},{10,1... | collective-permute-start | bytes 1671176 | tf_op jit(solution)/shard_map/back/return2/ppermute | solution.py:305
  333.2 40.2 %all-to-all-start.9 = ((bf16[32,144,128]{2,1,0:T(8,128)(2,1)}), bf16[32,144,128]{2,1,0:T(8,128)(2,1)}, u32[]{:S(2)}, u32[]{:S(2)}) async-start(bf16[32,144,128]{2,1,0:T(8,128)(2,1)} %copy-done.22), calls=%async_computation.9 | async-start | bytes 2359296 | tf_op jit(solution)/shard_map/back/all_to_all | solution.py:373
  343.8 16.3 %collective-permute-start.21 = (bf16[17,128,128]{2,1,0:T(8,128)(2,1)S(1)}, bf16[17,128,128]{2,1,0:T(8,128)(2,1)S(1)}, u32[]{:S(2)}, u32[]{:S(2)}) collective-permute-start(bf16[17,128,128]{2,1,0:T(8,128)(2,1)S(1)} %merge0.15), channel_id=1, source_target_pairs={{0,1},{1,2},{2,3},{3,4},{4,5},{5,6},{6,7},{7,0},{8,9},{9,10},{10,1... | collective-permute-start | bytes 1671176 | tf_op jit(solution)/shard_map/back/return1/ppermute | solution.py:305
  346.0 14.9 %collective-permute-start.22 = (bf16[17,128,128]{2,1,0:T(8,128)(2,1)S(1)}, bf16[17,128,128]{2,1,0:T(8,128)(2,1)S(1)}, u32[]{:S(2)}, u32[]{:S(2)}) collective-permute-start(bf16[17,128,128]{2,1,0:T(8,128)(2,1)S(1)} %merge1.10), channel_id=1, source_target_pairs={{0,7},{1,0},{2,1},{3,2},{4,3},{5,4},{6,5},{7,6},{8,15},{9,8},{10,9... | collective-permute-start | bytes 1671176 | tf_op jit(solution)/shard_map/back/return1/ppermute | solution.py:305
  350.3 22.3 %collective-permute-start.24 = (bf16[17,128,128]{2,1,0:T(8,128)(2,1)S(1)}, bf16[17,128,128]{2,1,0:T(8,128)(2,1)S(1)}, u32[]{:S(2)}, u32[]{:S(2)}) collective-permute-start(bf16[17,128,128]{2,1,0:T(8,128)(2,1)S(1)} %merge1.11), channel_id=1, source_target_pairs={{0,7},{1,0},{2,1},{3,2},{4,3},{5,4},{6,5},{7,6},{8,15},{9,8},{10,9... | collective-permute-start | bytes 1671176 | tf_op jit(solution)/shard_map/back/return1/ppermute | solution.py:305
  353.2 20.2 %collective-permute-start.23 = (bf16[17,128,128]{2,1,0:T(8,128)(2,1)S(1)}, bf16[17,128,128]{2,1,0:T(8,128)(2,1)S(1)}, u32[]{:S(2)}, u32[]{:S(2)}) collective-permute-start(bf16[17,128,128]{2,1,0:T(8,128)(2,1)S(1)} %merge0.16), channel_id=1, source_target_pairs={{0,1},{1,2},{2,3},{3,4},{4,5},{5,6},{6,7},{7,0},{8,9},{9,10},{10,1... | collective-permute-start | bytes 1671176 | tf_op jit(solution)/shard_map/back/return1/ppermute | solution.py:305
  (61 other events, 347.7 us)

commit v2 on v1

--- a/solution.py
+++ b/solution.py
@@ -387,25 +387,26 @@
         with jax.named_scope(f"own{c}"):
             return tuple(own(sources[c], CHUNKS[c], kv, info))
 
-    def merged(c, back, arrivals):
-        out = {}
+    def merged(c, back, arrivals, spans=((0, 8),)):
+        out = []
         with jax.named_scope(f"merge{c}"):
-            for low in (0, 4):
+            for span in spans:
                 for j, away_by in enumerate(CHUNKS[c]):
-                    coming = arrivals.get((j, low), [])
-                    coming = [(low, acc) for acc in coming]
-                    span = ((low, low + 4),)
-                    (out[j, low],) = merge(
-                        j, away_by, info, table, back, owns[c], coming, span
-                    )
+                    coming = [
+                        (low, acc)
+                        for (at, low, high), acc in arrivals
+                        if at == j and low < span[1] and high > span[0]
+                    ]
+                    (acc,) = merge(j, away_by, info, table, back, owns[c], coming, (span,))
+                    out.append(((j,) + span, acc))
         return out
 
     def onward(c, parts):
         with jax.named_scope(f"return{c}"):
-            return {(j, low): [ring(acc, 1 - 2 * j)] for (j, low), acc in parts.items()}
-
-    def arrived(arrivals):
-        return [acc for (acc,) in arrivals.values()]
+            return [(key, ring(acc, 1 - 2 * key[0])) for key, acc in parts]
+
+    def arrays(arrivals):
+        return [acc for _, acc in arrivals]
 
     with jax.named_scope("forward"):
         got0 = exchange(pack(sources[0], (0,), tile_of_mine), column, *sources[1])
@@ -421,15 +422,15 @@
     with jax.named_scope("back"):
         back4 = exchange(part4)
         back3 = exchange(part3)
-        parts = merged(4, back4, {})
-        arrivals = onward(4, {(0, 0): parts[0, 0], (1, 4): parts[0, 4]})
-        back2 = exchange(part2, part1, *arrived(arrivals))
+        (low, high) = merged(4, back4, [], ((0, 4), (4, 8)))
+        arrivals = onward(4, [((0, 0, 4), low[1]), ((1, 4, 8), high[1])])
+        back2 = exchange(part2, part1, *arrays(arrivals))
         arrivals = onward(3, merged(3, back3, arrivals))
-        back1 = exchange(part1, *arrived(arrivals))
+        back1 = exchange(part1, *arrays(arrivals))
         arrivals = onward(2, merged(2, back2, arrivals))
-        back0 = exchange(part0, *arrived(arrivals))
+        back0 = exchange(part0)
         arrivals = onward(1, merged(1, back1, arrivals))
-        arrivals = [(low, acc) for (_, low), (acc,) in arrivals.items()]
+        arrivals = [(low, acc) for (_, low, _), acc in arrivals]
         return merge(0, 0, info, table, back0, own0, arrivals, None)[0]
 
 

time: 384 us -> 378 us (0.984)
  local copies, waits for them, and re-layouts: 54.5 us -> 40.2 us
  waiting for transfers between devices: 118 us -> 131 us
  starting transfers between devices: 113 us -> 107 us
    all_to_all x9, waiting for transfers between devices: 34.9 us -> 53.2 us  [exchange(): got = lax.all_to_all(send, ('y', 'c', 'x'), 0, 0, tiled=True)]
    unnamed x121 -> x83, local copies, waits for them, and re-layouts: 47.5 us -> 33 us
    ppermute x25 -> x19, waiting for transfers between devices: 81.3 us -> 75.3 us  [ring(): return lax.ppermute(x, axis, [(i, (i + step) % size) for i in range(size)])]
    ppermute x25 -> x19, starting transfers between devices: 37.4 us -> 32.5 us  [ring(): return lax.ppermute(x, axis, [(i, (i + step) % size) for i in range(size)])]
    pallas_call x15 -> x9, Pallas kernels: 25.8 us -> 26.2 us  [merge(): pl.pallas_call(functools.partial(merge_kernel, j, away, places, spans), o...]
  transfers between devices with their start and end apart: 35 -> 29, of which waited for: 15 -> 14; matrix products, arithmetic and copies ran while one was open for 4% -> 4% of each run, Pallas kernels for 21% -> 22%
where the time goes in v2:
time: 378 us; the launch traced here: 376 us
  waiting for transfers between devices  131 us (35%)
  starting transfers between devices  107 us (28%)
  Pallas kernels  95.1 us (25%)
  local copies, waits for them, and re-layouts  40.2 us (11%)
    ppermute x19, waiting for transfers between devices, ring(): return lax.ppermute(x, axis, [(i, (i + step) % size) for i in range(size)])  75.3 us
    all_to_all x9, starting transfers between devices, exchange(): got = lax.all_to_all(send, ('y', 'c', 'x'), 0, 0, tiled=True)  69.2 us
    all_to_all x9, waiting for transfers between devices, exchange(): got = lax.all_to_all(send, ('y', 'c', 'x'), 0, 0, tiled=True)  53.2 us
    pallas_call x5, Pallas kernels, far(): pl.pallas_call(functools.partial(far_kernel, aways, first), out_shape=jax...  43.6 us
    unnamed x83, local copies, waits for them, and re-layouts  33 us
    ppermute x19, starting transfers between devices, ring(): return lax.ppermute(x, axis, [(i, (i + step) % size) for i in range(size)])  32.5 us
    pallas_call x9, Pallas kernels, merge(): pl.pallas_call(functools.partial(merge_kernel, j, away, places, spans), o...  26.2 us
    pallas_call x5, Pallas kernels, own(): pl.pallas_call(functools.partial(own_kernel, aways), out_shape=(jax.Shape...  16.9 us
  transfers between devices with their start and end apart: 29, of which 14 were waited for; matrix products, arithmetic and copies ran while one was open for 4% of the time, Pallas kernels for 22%

profile of v2, /device:TPU:1, one launch (start us, length us, event | category | flops | bytes accessed | tf_op | source)
XLA Modules:
  0.0 376.4 jit_solution(7363962102838797866)
XLA Ops:
  4.2 4.0 %collective-permute-start = (bf16[32,128,128]{2,1,0:T(8,128)(2,1)S(1)}, bf16[32,128,128]{2,1,0:T(8,128)(2,1)}, u32[]{:S(2)}, u32[]{:S(2)}) collective-permute-start(bf16[32,128,128]{2,1,0:T(8,128)(2,1)S(1)} %bitcast.52), channel_id=1, source_target_pairs={{0,7},{1,0},{2,1},{3,2},{4,3},{5,4},{6,5},{7,6},{8,15},{9,8},{10,9... | collective-permute-start | bytes 3145736 | tf_op jit(solution)/shard_map/ring1/ppermute | solution.py:305
  9.1 5.2 %all-to-all-start = ((s32[8,1,128]{2,1,0:T(1,128)}), s32[8,1,128]{2,1,0:T(1,128)S(1)}, u32[]{:S(2)}, u32[]{:S(2)}) async-start(s32[8,1,128]{2,1,0:T(1,128)} %broadcast_in_dim.61), calls=%async_computation | async-start | bytes 8192 | tf_op jit(solution)/shard_map/column/all_to_all | solution.py:324
  23.3 6.5 %copy.24 = bf16[2048,1024]{0,1:T(8,128)(2,1)} copy(bf16[2048,1024]{1,0:T(8,128)(2,1)} %param.10) | data formatting | bytes 8388608 | tf_op args[4]
  33.9 9.0 %all-to-all-start.1 = ((bf16[32,128,128]{2,1,0:T(8,128)(2,1)}), bf16[32,128,128]{2,1,0:T(8,128)(2,1)}, u32[]{:S(2)}, u32[]{:S(2)}) async-start(bf16[32,128,128]{2,1,0:T(8,128)(2,1)} %copy-done.18), calls=%async_computation.1 | async-start | bytes 2097152 | tf_op jit(solution)/shard_map/forward/all_to_all | solution.py:373
  51.2 4.4 %own2.3 = (bf16[32,128,128]{2,1,0:T(8,128)(2,1)S(1)}, f32[8,4,128]{2,1,0:T(4,128)S(1)}) custom-call(s32[128]{0:T(128)S(1)} %compare_select_fusion.5.info_ref, bf16[4,4,128,128]{3,2,1,0:T(8,128)(2,1)S(1)} %pad_maximum_fusion.kv_ref, bf16[32,128,128]{2,1,0:T(8,128)(2,1)} %collective-permute-done.refs_0_, bf16[32,128,128]{2,1,0:T(8,128)(2,1)S(1)} %collective-permute-done.1.refs_1_), custom_call_target="tpu_custom_call" | custom-call | flops 268435456 | bytes 4194304 | tf_op jit(solution)/shard_map/forward/own1/own2/pallas_call | solution.py:188
  59.0 5.5 %all-to-all-start.2 = ((s32[32,1,128]{2,1,0:T(1,128)}), s32[32,1,128]{2,1,0:T(1,128)S(1)}, u32[]{:S(2)}, u32[]{:S(2)}) async-start(s32[32,1,128]{2,1,0:T(1,128)} %bitcast.20), calls=%async_computation.2 | async-start | bytes 32768 | tf_op jit(solution)/shard_map/forward/all_to_all | solution.py:373
  64.4 4.3 %collective-permute-done.6.refs_3_.refs_1_ = bf16[32,128,128]{2,1,0:T(8,128)(2,1)} collective-permute-done((bf16[32,128,128]{2,1,0:T(8,128)(2,1)S(1)}, bf16[32,128,128]{2,1,0:T(8,128)(2,1)}, u32[]{:S(2)}, u32[]{:S(2)}) %collective-permute-start.6) | collective-permute-done | bytes 1048608 | tf_op jit(solution)/shard_map/ring2/ppermute | solution.py:305
  69.7 4.0 %pack4.1 = bf16[32,512,128]{2,1,0:T(8,128)(2,1)} custom-call(s32[256]{0:T(256)S(1)} %add_select_fusion.8.idx_ref, bf16[32,128,128]{2,1,0:T(8,128)(2,1)} %collective-permute-done.refs_0_, bf16[32,128,128]{2,1,0:T(8,128)(2,1)S(1)} %collective-permute-done.1.refs_1_, bf16[32,128,128]{2,1,0:T(8,128)(2,1)} %collective-permute-done.5.refs_2_.refs_0_, ...), custom_call_target="tpu_custom_call" | custom-call | bytes 8388608 | tf_op jit(solution)/shard_map/forward/pack4/pallas_call | solution.py:57
  73.6 8.5 %all-to-all-start.3 = ((bf16[32,512,128]{2,1,0:T(8,128)(2,1)}), bf16[32,512,128]{2,1,0:T(8,128)(2,1)}, u32[]{:S(2)}, u32[]{:S(2)}) async-start(bf16[32,512,128]{2,1,0:T(8,128)(2,1)} %pack4.1), calls=%async_computation.3 | async-start | bytes 8388608 | tf_op jit(solution)/shard_map/forward/all_to_all | solution.py:373
  84.9 23.3 %collective-permute-done.8.refs_1_ = bf16[32,128,128]{2,1,0:T(8,128)(2,1)S(1)} collective-permute-done((bf16[32,128,128]{2,1,0:T(8,128)(2,1)}, bf16[32,128,128]{2,1,0:T(8,128)(2,1)S(1)}, u32[]{:S(2)}, u32[]{:S(2)}) %collective-permute-start.8) | collective-permute-done | bytes 1048608 | tf_op jit(solution)/shard_map/ring3/ppermute | solution.py:305
  112.8 8.2 %far1.2 = bf16[32,144,128]{2,1,0:T(8,128)(2,1)} custom-call(s32[256]{0:T(256)S(1)} %reshape.340.meta_ref, bf16[32,128,128]{2,1,0:T(8,128)(2,1)} %all-to-all-done.1.got_ref, bf16[2048,1024]{1,0:T(8,128)(2,1)} %k_ref.9, bf16[1024,2048]{1,0:T(8,128)(2,1)} %bitcast.55), custom_call_target="tpu_custom_call" | custom-call | flops 1073741824 | bytes 12582912 | tf_op jit(solution)/shard_map/forward/far0/far1/pallas_call | solution.py:132
  121.0 4.7 %own2.4 = (bf16[32,128,128]{2,1,0:T(8,128)(2,1)S(1)}, f32[8,4,128]{2,1,0:T(4,128)S(1)}) custom-call(s32[128]{0:T(128)S(1)} %compare_select_fusion.5.info_ref, bf16[4,4,128,128]{3,2,1,0:T(8,128)(2,1)S(1)} %pad_maximum_fusion.kv_ref, bf16[32,128,128]{2,1,0:T(8,128)(2,1)} %collective-permute-done.5.refs_2_.refs_0_, ...), custom_call_target="tpu_custom_call" | custom-call | flops 268435456 | bytes 4194304 | tf_op jit(solution)/shard_map/forward/own2/own2/pallas_call | solution.py:188
  131.8 10.4 %all-to-all-start.4 = ((bf16[32,384,128]{2,1,0:T(8,128)(2,1)}), bf16[32,384,128]{2,1,0:T(8,128)(2,1)S(1)}, u32[]{:S(2)}, u32[]{:S(2)}) async-start(bf16[32,384,128]{2,1,0:T(8,128)(2,1)} %pack3.1), calls=%async_computation.4 | async-start | bytes 6291456 | tf_op jit(solution)/shard_map/forward/all_to_all | solution.py:373
  145.7 3.7 own2.5
  152.3 9.2 %far2.4 = bf16[32,272,128]{2,1,0:T(8,128)(2,1)S(1)} custom-call(s32[256]{0:T(256)S(1)} %reshape.340.meta_ref, bf16[32,512,128]{2,1,0:T(8,128)(2,1)} %all-to-all-done.3.got_ref, bf16[2048,1024]{1,0:T(8,128)(2,1)} %k_ref.9, bf16[1024,2048]{1,0:T(8,128)(2,1)} %bitcast.56), custom_call_target="tpu_custom_call" | custom-call | flops 2147483648 | bytes 12582912 | tf_op jit(solution)/shard_map/forward/far2/far2/pallas_call | solution.py:132
  162.8 17.3 %all-to-all-done.4.got_ref = bf16[32,384,128]{2,1,0:T(8,128)(2,1)S(1)} async-done(((bf16[32,384,128]{2,1,0:T(8,128)(2,1)}), bf16[32,384,128]{2,1,0:T(8,128)(2,1)S(1)}, u32[]{:S(2)}, u32[]{:S(2)}) %all-to-all-start.4) | async-done | bytes 3145760 | tf_op jit(solution)/shard_map/forward/all_to_all | solution.py:373
  180.1 7.1 %far1.3 = bf16[32,144,128]{2,1,0:T(8,128)(2,1)S(1)} custom-call(s32[256]{0:T(256)S(1)} %reshape.340.meta_ref, bf16[32,384,128]{2,1,0:T(8,128)(2,1)S(1)} %all-to-all-done.4.got_ref, bf16[2048,1024]{1,0:T(8,128)(2,1)} %k_ref.9, bf16[1024,2048]{1,0:T(8,128)(2,1)} %bitcast.57), custom_call_target="tpu_custom_call" | custom-call | flops 1073741824 | bytes 12582912 | tf_op jit(solution)/shard_map/forward/far4/far1/pallas_call | solution.py:132
  188.3 8.6 %all-to-all-start.5 = ((bf16[32,144,128]{2,1,0:T(8,128)(2,1)}), bf16[32,144,128]{2,1,0:T(8,128)(2,1)}, u32[]{:S(2)}, u32[]{:S(2)}) async-start(bf16[32,144,128]{2,1,0:T(8,128)(2,1)} %copy-done.13), calls=%async_computation.5 | async-start | bytes 2359296 | tf_op jit(solution)/shard_map/back/all_to_all | solution.py:373
  196.9 8.7 %far2.5 = bf16[32,272,128]{2,1,0:T(8,128)(2,1)S(1)} custom-call(s32[256]{0:T(256)S(1)} %reshape.340.meta_ref, bf16[32,384,128]{2,1,0:T(8,128)(2,1)S(1)} %all-to-all-done.4.got_ref, bf16[2048,1024]{1,0:T(8,128)(2,1)} %k_ref.9, bf16[1024,2048]{1,0:T(8,128)(2,1)} %bitcast.58), custom_call_target="tpu_custom_call" | custom-call | flops 2147483648 | bytes 12582912 | tf_op jit(solution)/shard_map/forward/far3/far2/pallas_call | solution.py:132
  207.0 7.3 %all-to-all-done.5.back_ref = bf16[32,144,128]{2,1,0:T(8,128)(2,1)} async-done(((bf16[32,144,128]{2,1,0:T(8,128)(2,1)}), bf16[32,144,128]{2,1,0:T(8,128)(2,1)}, u32[]{:S(2)}, u32[]{:S(2)}) %all-to-all-start.5) | async-done | bytes 1179680 | tf_op jit(solution)/shard_map/back/all_to_all | solution.py:373
  214.3 7.4 %all-to-all-start.6 = ((bf16[32,272,128]{2,1,0:T(8,128)(2,1)}), bf16[32,272,128]{2,1,0:T(8,128)(2,1)S(1)}, u32[]{:S(2)}, u32[]{:S(2)}) async-start(bf16[32,272,128]{2,1,0:T(8,128)(2,1)} %copy-done.4), calls=%async_computation.6 | async-start | bytes 4456448 | tf_op jit(solution)/shard_map/back/all_to_all | solution.py:373
  228.5 10.5 %far2.3 = bf16[32,272,128]{2,1,0:T(8,128)(2,1)S(1)} custom-call(s32[256]{0:T(256)S(1)} %reshape.340.meta_ref, bf16[32,512,128]{2,1,0:T(8,128)(2,1)} %all-to-all-done.3.got_ref, bf16[2048,1024]{1,0:T(8,128)(2,1)} %k_ref.9, bf16[1024,2048]{1,0:T(8,128)(2,1)} %bitcast.59), custom_call_target="tpu_custom_call" | custom-call | flops 2147483648 | bytes 12582912 | tf_op jit(solution)/shard_map/forward/far1/far2/pallas_call | solution.py:132
  242.0 7.9 %all-to-all-done.6.back_ref = bf16[32,272,128]{2,1,0:T(8,128)(2,1)S(1)} async-done(((bf16[32,272,128]{2,1,0:T(8,128)(2,1)}), bf16[32,272,128]{2,1,0:T(8,128)(2,1)S(1)}, u32[]{:S(2)}, u32[]{:S(2)}) %all-to-all-start.6) | async-done | bytes 2228256 | tf_op jit(solution)/shard_map/back/all_to_all | solution.py:373
  251.4 5.8 %all-to-all-start.7 = ((bf16[32,272,128]{2,1,0:T(8,128)(2,1)}), bf16[32,272,128]{2,1,0:T(8,128)(2,1)S(1)}, u32[]{:S(2)}, u32[]{:S(2)}) async-start(bf16[32,272,128]{2,1,0:T(8,128)(2,1)} %copy-done.5), calls=%async_computation.7 | async-start | bytes 4456448 | tf_op jit(solution)/shard_map/back/all_to_all | solution.py:373
  267.7 21.1 %collective-permute-done.13.refs_0_ = bf16[33,128,128]{2,1,0:T(8,128)(2,1)S(1)} collective-permute-done((bf16[33,128,128]{2,1,0:T(8,128)(2,1)S(1)}, bf16[33,128,128]{2,1,0:T(8,128)(2,1)S(1)}, u32[]{:S(2)}, u32[]{:S(2)}) %collective-permute-start.13) | collective-permute-done | bytes 1081376 | tf_op jit(solution)/shard_map/back/return3/ppermute | solution.py:305
  291.4 8.4 %all-to-all-start.8 = ((bf16[32,272,128]{2,1,0:T(8,128)(2,1)}), bf16[32,272,128]{2,1,0:T(8,128)(2,1)}, u32[]{:S(2)}, u32[]{:S(2)}) async-start(bf16[32,272,128]{2,1,0:T(8,128)(2,1)} %copy-done.6), calls=%async_computation.8 | async-start | bytes 4456448 | tf_op jit(solution)/shard_map/back/all_to_all | solution.py:373
  311.2 16.9 %all-to-all-done.8.back_ref = bf16[32,272,128]{2,1,0:T(8,128)(2,1)} async-done(((bf16[32,272,128]{2,1,0:T(8,128)(2,1)}), bf16[32,272,128]{2,1,0:T(8,128)(2,1)}, u32[]{:S(2)}, u32[]{:S(2)}) %all-to-all-start.8) | async-done | bytes 2228256 | tf_op jit(solution)/shard_map/back/all_to_all | solution.py:373
  328.1 5.5 %all-to-all-start.9 = ((bf16[32,144,128]{2,1,0:T(8,128)(2,1)}), bf16[32,144,128]{2,1,0:T(8,128)(2,1)S(1)}, u32[]{:S(2)}, u32[]{:S(2)}) async-start(bf16[32,144,128]{2,1,0:T(8,128)(2,1)} %far1.2), calls=%async_computation.9 | async-start | bytes 2359296 | tf_op jit(solution)/shard_map/back/all_to_all | solution.py:373
  333.6 3.6 merge1.5
  344.1 19.6 %collective-permute-done.18.refs_1_ = bf16[33,128,128]{2,1,0:T(8,128)(2,1)S(1)} collective-permute-done((bf16[33,128,128]{2,1,0:T(8,128)(2,1)S(1)}, bf16[33,128,128]{2,1,0:T(8,128)(2,1)S(1)}, u32[]{:S(2)}, u32[]{:S(2)}) %collective-permute-start.18) | collective-permute-done | bytes 1081376 | tf_op jit(solution)/shard_map/back/return1/ppermute | solution.py:305
  364.7 5.5 %collective-permute-done.16.refs_0_ = bf16[33,128,128]{2,1,0:T(8,128)(2,1)S(1)} collective-permute-done((bf16[33,128,128]{2,1,0:T(8,128)(2,1)S(1)}, bf16[33,128,128]{2,1,0:T(8,128)(2,1)S(1)}, u32[]{:S(2)}, u32[]{:S(2)}) %collective-permute-start.16) | collective-permute-done | bytes 1081376 | tf_op jit(solution)/shard_map/back/return1/ppermute | solution.py:305
  372.5 3.9 %merge0.11 = bf16[4096,128]{1,0:T(8,128)(2,1)} custom-call(s32[128]{0:T(128)S(1)} %compare_select_fusion.5.info_ref, s32[1024]{0:T(1024)S(1)} %fusion.18.table_ref, bf16[32,144,128]{2,1,0:T(8,128)(2,1)S(1)} %all-to-all-done.9.back_ref, bf16[16,128,128]{2,1,0:T(8,128)(2,1)S(1)} %copy-done.34, f32[4,4,128]{2,1,0:T(4,128)S(1)} %get-tuple-element.34.own_lse_ref, ...), custom_call_target="tpu_custom_call" | custom-call | flops 6291456 | bytes 4194304 | tf_op jit(solution)/shard_map/back/merge0/pallas_call | solution.py:287
  (162 shorter events, 99.9 us)
Async XLA Ops:
  1.7 32.2 %collective-permute-start.1 = (bf16[32,128,128]{2,1,0:T(8,128)(2,1)S(1)}, bf16[32,128,128]{2,1,0:T(8,128)(2,1)S(1)}, u32[]{:S(2)}, u32[]{:S(2)}) collective-permute-start(bf16[32,128,128]{2,1,0:T(8,128)(2,1)S(1)} %bitcast.51), channel_id=1, source_target_pairs={{0,1},{1,2},{2,3},{3,4},{4,5},{5,6},{6,7},{7,0},{8,9},{9,10},{10,1... | collective-permute-start | bytes 3145736 | tf_op jit(solution)/shard_map/ring1/ppermute | solution.py:305
  4.2 29.6 %collective-permute-start = (bf16[32,128,128]{2,1,0:T(8,128)(2,1)S(1)}, bf16[32,128,128]{2,1,0:T(8,128)(2,1)}, u32[]{:S(2)}, u32[]{:S(2)}) collective-permute-start(bf16[32,128,128]{2,1,0:T(8,128)(2,1)S(1)} %bitcast.52), channel_id=1, source_target_pairs={{0,7},{1,0},{2,1},{3,2},{4,3},{5,4},{6,5},{7,6},{8,15},{9,8},{10,9... | collective-permute-start | bytes 3145736 | tf_op jit(solution)/shard_map/ring1/ppermute | solution.py:305
  9.1 23.5 %all-to-all-start = ((s32[8,1,128]{2,1,0:T(1,128)}), s32[8,1,128]{2,1,0:T(1,128)S(1)}, u32[]{:S(2)}, u32[]{:S(2)}) async-start(s32[8,1,128]{2,1,0:T(1,128)} %broadcast_in_dim.61), calls=%async_computation | async-start | bytes 8192 | tf_op jit(solution)/shard_map/column/all_to_all | solution.py:324
  14.9 31.7 %collective-permute-start.2 = (bf16[4,128,128]{2,1,0:T(8,128)(2,1)S(1)}, bf16[4,128,128]{2,1,0:T(8,128)(2,1)S(1)}, u32[]{:S(2)}, u32[]{:S(2)}) collective-permute-start(bf16[4,128,128]{2,1,0:T(8,128)(2,1)S(1)} %get-tuple-element.56), channel_id=1, source_target_pairs={{0,8},{8,16},{16,24},{24,0},{1,9},{9,17},{17,25},{25,1},{2,10},{10... | collective-permute-start | bytes 393224 | tf_op jit(solution)/shard_map/kv/ppermute | solution.py:305
  16.2 30.4 %collective-permute-start.3 = (bf16[4,128,128]{2,1,0:T(8,128)(2,1)S(1)}, bf16[4,128,128]{2,1,0:T(8,128)(2,1)S(1)}, u32[]{:S(2)}, u32[]{:S(2)}) collective-permute-start(bf16[4,128,128]{2,1,0:T(8,128)(2,1)S(1)} %get-tuple-element.57), channel_id=1, source_target_pairs={{0,16},{8,24},{16,0},{24,8},{1,17},{9,25},{17,1},{25,9},{2,18},{10... | collective-permute-start | bytes 393224 | tf_op jit(solution)/shard_map/kv/ppermute | solution.py:305
  18.6 28.0 %collective-permute-start.4 = (bf16[4,128,128]{2,1,0:T(8,128)(2,1)S(1)}, bf16[4,128,128]{2,1,0:T(8,128)(2,1)S(1)}, u32[]{:S(2)}, u32[]{:S(2)}) collective-permute-start(bf16[4,128,128]{2,1,0:T(8,128)(2,1)S(1)} %get-tuple-element.58), channel_id=1, source_target_pairs={{0,24},{8,0},{16,8},{24,16},{1,25},{9,1},{17,9},{25,17},{2,26},{10... | collective-permute-start | bytes 393224 | tf_op jit(solution)/shard_map/kv/ppermute | solution.py:305
  33.9 25.1 %all-to-all-start.1 = ((bf16[32,128,128]{2,1,0:T(8,128)(2,1)}), bf16[32,128,128]{2,1,0:T(8,128)(2,1)}, u32[]{:S(2)}, u32[]{:S(2)}) async-start(bf16[32,128,128]{2,1,0:T(8,128)(2,1)} %copy-done.18), calls=%async_computation.1 | async-start | bytes 2097152 | tf_op jit(solution)/shard_map/forward/all_to_all | solution.py:373
  42.9 25.8 %collective-permute-start.6 = (bf16[32,128,128]{2,1,0:T(8,128)(2,1)S(1)}, bf16[32,128,128]{2,1,0:T(8,128)(2,1)}, u32[]{:S(2)}, u32[]{:S(2)}) collective-permute-start(bf16[32,128,128]{2,1,0:T(8,128)(2,1)S(1)} %collective-permute-done.1.refs_1_), channel_id=1, source_target_pairs={{0,1},{1,2},{2,3},{3,4},{4,5},{5,6},{6,7},{7,0},{8,9},{9,10},{10,1... | collective-permute-start | bytes 3145736 | tf_op jit(solution)/shard_map/ring2/ppermute | solution.py:305
  45.2 24.4 %collective-permute-start.5 = (bf16[32,128,128]{2,1,0:T(8,128)(2,1)}, bf16[32,128,128]{2,1,0:T(8,128)(2,1)}, u32[]{:S(2)}, u32[]{:S(2)}) collective-permute-start(bf16[32,128,128]{2,1,0:T(8,128)(2,1)} %collective-permute-done.refs_0_), channel_id=1, source_target_pairs={{0,7},{1,0},{2,1},{3,2},{4,3},{5,4},{6,5},{7,6},{8,15},{9,8},{10,9... | collective-permute-start | bytes 3145736 | tf_op jit(solution)/shard_map/ring2/ppermute | solution.py:305
  48.3 72.7 %copy-start.2 = (bf16[4,4,128,128]{3,2,1,0:T(8,128)(2,1)}, bf16[4,4,128,128]{3,2,1,0:T(8,128)(2,1)S(1)}, u32[]{:S(2)}) copy-start(bf16[4,4,128,128]{3,2,1,0:T(8,128)(2,1)S(1)} %pad_maximum_fusion.kv_ref) | copy-start | bytes 1572868
  59.0 14.7 %all-to-all-start.2 = ((s32[32,1,128]{2,1,0:T(1,128)}), s32[32,1,128]{2,1,0:T(1,128)S(1)}, u32[]{:S(2)}, u32[]{:S(2)}) async-start(s32[32,1,128]{2,1,0:T(1,128)} %bitcast.20), calls=%async_computation.2 | async-start | bytes 32768 | tf_op jit(solution)/shard_map/forward/all_to_all | solution.py:373
  73.6 58.1 %all-to-all-start.3 = ((bf16[32,512,128]{2,1,0:T(8,128)(2,1)}), bf16[32,512,128]{2,1,0:T(8,128)(2,1)}, u32[]{:S(2)}, u32[]{:S(2)}) async-start(bf16[32,512,128]{2,1,0:T(8,128)(2,1)} %pack4.1), calls=%async_computation.3 | async-start | bytes 8388608 | tf_op jit(solution)/shard_map/forward/all_to_all | solution.py:373
  82.2 26.0 %collective-permute-start.8 = (bf16[32,128,128]{2,1,0:T(8,128)(2,1)}, bf16[32,128,128]{2,1,0:T(8,128)(2,1)S(1)}, u32[]{:S(2)}, u32[]{:S(2)}) collective-permute-start(bf16[32,128,128]{2,1,0:T(8,128)(2,1)} %collective-permute-done.6.refs_3_.refs_1_), channel_id=1, source_target_pairs={{0,1},{1,2},{2,3},{3,4},{4,5},{5,6},{6,7},{7,0},{8,9},{9,10},{10,1... | collective-permute-start | bytes 3145736 | tf_op jit(solution)/shard_map/ring3/ppermute | solution.py:305
  82.5 26.6 %collective-permute-start.7 = (bf16[32,128,128]{2,1,0:T(8,128)(2,1)}, bf16[32,128,128]{2,1,0:T(8,128)(2,1)S(1)}, u32[]{:S(2)}, u32[]{:S(2)}) collective-permute-start(bf16[32,128,128]{2,1,0:T(8,128)(2,1)} %collective-permute-done.5.refs_2_.refs_0_), channel_id=1, source_target_pairs={{0,7},{1,0},{2,1},{3,2},{4,3},{5,4},{6,5},{7,6},{8,15},{9,8},{10,9... | collective-permute-start | bytes 3145736 | tf_op jit(solution)/shard_map/ring3/ppermute | solution.py:305
  109.1 16.5 %collective-permute-start.9 = (bf16[16,128,128]{2,1,0:T(8,128)(2,1)}, bf16[16,128,128]{2,1,0:T(8,128)(2,1)S(1)}, u32[]{:S(2)}, u32[]{:S(2)}) collective-permute-start(bf16[16,128,128]{2,1,0:T(8,128)(2,1)} %slice.15), channel_id=1, source_target_pairs={{0,1},{1,2},{2,3},{3,4},{4,5},{5,6},{6,7},{7,0},{8,9},{9,10},{10,1... | collective-permute-start | bytes 1572872 | tf_op jit(solution)/shard_map/ring4/ppermute | solution.py:305
  110.1 15.7 %collective-permute-start.10 = (bf16[16,128,128]{2,1,0:T(8,128)(2,1)}, bf16[16,128,128]{2,1,0:T(8,128)(2,1)}, u32[]{:S(2)}, u32[]{:S(2)}) collective-permute-start(bf16[16,128,128]{2,1,0:T(8,128)(2,1)} %slice.16), channel_id=1, source_target_pairs={{0,7},{1,0},{2,1},{3,2},{4,3},{5,4},{6,5},{7,6},{8,15},{9,8},{10,9... | collective-permute-start | bytes 1572872 | tf_op jit(solution)/shard_map/ring4/ppermute | solution.py:305
  131.8 48.4 %all-to-all-start.4 = ((bf16[32,384,128]{2,1,0:T(8,128)(2,1)}), bf16[32,384,128]{2,1,0:T(8,128)(2,1)S(1)}, u32[]{:S(2)}, u32[]{:S(2)}) async-start(bf16[32,384,128]{2,1,0:T(8,128)(2,1)} %pack3.1), calls=%async_computation.4 | async-start | bytes 6291456 | tf_op jit(solution)/shard_map/forward/all_to_all | solution.py:373
  188.3 26.0 %all-to-all-start.5 = ((bf16[32,144,128]{2,1,0:T(8,128)(2,1)}), bf16[32,144,128]{2,1,0:T(8,128)(2,1)}, u32[]{:S(2)}, u32[]{:S(2)}) async-start(bf16[32,144,128]{2,1,0:T(8,128)(2,1)} %copy-done.13), calls=%async_computation.5 | async-start | bytes 2359296 | tf_op jit(solution)/shard_map/back/all_to_all | solution.py:373
  214.3 35.7 %all-to-all-start.6 = ((bf16[32,272,128]{2,1,0:T(8,128)(2,1)}), bf16[32,272,128]{2,1,0:T(8,128)(2,1)S(1)}, u32[]{:S(2)}, u32[]{:S(2)}) async-start(bf16[32,272,128]{2,1,0:T(8,128)(2,1)} %copy-done.4), calls=%async_computation.6 | async-start | bytes 4456448 | tf_op jit(solution)/shard_map/back/all_to_all | solution.py:373
  223.7 15.3 %collective-permute-start.11 = (bf16[17,128,128]{2,1,0:T(8,128)(2,1)S(1)}, bf16[17,128,128]{2,1,0:T(8,128)(2,1)S(1)}, u32[]{:S(2)}, u32[]{:S(2)}) collective-permute-start(bf16[17,128,128]{2,1,0:T(8,128)(2,1)S(1)} %merge0.6), channel_id=1, source_target_pairs={{0,1},{1,2},{2,3},{3,4},{4,5},{5,6},{6,7},{7,0},{8,9},{9,10},{10,1... | collective-permute-start | bytes 1671176 | tf_op jit(solution)/shard_map/back/return4/ppermute | solution.py:305
  225.8 15.4 %collective-permute-start.12 = (bf16[17,128,128]{2,1,0:T(8,128)(2,1)S(1)}, bf16[17,128,128]{2,1,0:T(8,128)(2,1)S(1)}, u32[]{:S(2)}, u32[]{:S(2)}) collective-permute-start(bf16[17,128,128]{2,1,0:T(8,128)(2,1)S(1)} %merge0.7), channel_id=1, source_target_pairs={{0,7},{1,0},{2,1},{3,2},{4,3},{5,4},{6,5},{7,6},{8,15},{9,8},{10,9... | collective-permute-start | bytes 1671176 | tf_op jit(solution)/shard_map/back/return4/ppermute | solution.py:305
  251.4 40.0 %all-to-all-start.7 = ((bf16[32,272,128]{2,1,0:T(8,128)(2,1)}), bf16[32,272,128]{2,1,0:T(8,128)(2,1)S(1)}, u32[]{:S(2)}, u32[]{:S(2)}) async-start(bf16[32,272,128]{2,1,0:T(8,128)(2,1)} %copy-done.5), calls=%async_computation.7 | async-start | bytes 4456448 | tf_op jit(solution)/shard_map/back/all_to_all | solution.py:373
  262.2 26.5 %collective-permute-start.13 = (bf16[33,128,128]{2,1,0:T(8,128)(2,1)S(1)}, bf16[33,128,128]{2,1,0:T(8,128)(2,1)S(1)}, u32[]{:S(2)}, u32[]{:S(2)}) collective-permute-start(bf16[33,128,128]{2,1,0:T(8,128)(2,1)S(1)} %merge0.8), channel_id=1, source_target_pairs={{0,1},{1,2},{2,3},{3,4},{4,5},{5,6},{6,7},{7,0},{8,9},{9,10},{10,1... | collective-permute-start | bytes 3244040 | tf_op jit(solution)/shard_map/back/return3/ppermute | solution.py:305
  264.7 35.1 %copy-start.17 = (bf16[32,128,128]{2,1,0:T(8,128)(2,1)S(1)}, bf16[32,128,128]{2,1,0:T(8,128)(2,1)}, u32[]{:S(2)}) copy-start(bf16[32,128,128]{2,1,0:T(8,128)(2,1)} %copy-done.16) | copy-start | bytes 3145732
  264.7 25.7 %collective-permute-start.14 = (bf16[33,128,128]{2,1,0:T(8,128)(2,1)S(1)}, bf16[33,128,128]{2,1,0:T(8,128)(2,1)S(1)}, u32[]{:S(2)}, u32[]{:S(2)}) collective-permute-start(bf16[33,128,128]{2,1,0:T(8,128)(2,1)S(1)} %merge1.3), channel_id=1, source_target_pairs={{0,7},{1,0},{2,1},{3,2},{4,3},{5,4},{6,5},{7,6},{8,15},{9,8},{10,9... | collective-permute-start | bytes 3244040 | tf_op jit(solution)/shard_map/back/return3/ppermute | solution.py:305
  291.4 36.7 %all-to-all-start.8 = ((bf16[32,272,128]{2,1,0:T(8,128)(2,1)}), bf16[32,272,128]{2,1,0:T(8,128)(2,1)}, u32[]{:S(2)}, u32[]{:S(2)}) async-start(bf16[32,272,128]{2,1,0:T(8,128)(2,1)} %copy-done.6), calls=%async_computation.8 | async-start | bytes 4456448 | tf_op jit(solution)/shard_map/back/all_to_all | solution.py:373
  304.5 29.1 %collective-permute-start.17 = (bf16[33,128,128]{2,1,0:T(8,128)(2,1)}, bf16[33,128,128]{2,1,0:T(8,128)(2,1)}, u32[]{:S(2)}, u32[]{:S(2)}) collective-permute-start(bf16[33,128,128]{2,1,0:T(8,128)(2,1)} %merge1.4), channel_id=1, source_target_pairs={{0,7},{1,0},{2,1},{3,2},{4,3},{5,4},{6,5},{7,6},{8,15},{9,8},{10,9... | collective-permute-start | bytes 3244040 | tf_op jit(solution)/shard_map/back/return2/ppermute | solution.py:305
  311.2 22.4 %copy-start.15 = (bf16[32,128,128]{2,1,0:T(8,128)(2,1)S(1)}, bf16[32,128,128]{2,1,0:T(8,128)(2,1)}, u32[]{:S(2)}) copy-start(bf16[32,128,128]{2,1,0:T(8,128)(2,1)} %copy-done.14) | copy-start | bytes 3145732
  311.2 29.5 %collective-permute-start.15 = (bf16[33,128,128]{2,1,0:T(8,128)(2,1)}, bf16[33,128,128]{2,1,0:T(8,128)(2,1)S(1)}, u32[]{:S(2)}, u32[]{:S(2)}) collective-permute-start(bf16[33,128,128]{2,1,0:T(8,128)(2,1)} %merge0.9), channel_id=1, source_target_pairs={{0,1},{1,2},{2,3},{3,4},{4,5},{5,6},{6,7},{7,0},{8,9},{9,10},{10,1... | collective-permute-start | bytes 3244040 | tf_op jit(solution)/shard_map/back/return2/ppermute | solution.py:305
  328.1 42.2 %all-to-all-start.9 = ((bf16[32,144,128]{2,1,0:T(8,128)(2,1)}), bf16[32,144,128]{2,1,0:T(8,128)(2,1)S(1)}, u32[]{:S(2)}, u32[]{:S(2)}) async-start(bf16[32,144,128]{2,1,0:T(8,128)(2,1)} %far1.2), calls=%async_computation.9 | async-start | bytes 2359296 | tf_op jit(solution)/shard_map/back/all_to_all | solution.py:373
  337.2 26.5 %collective-permute-start.18 = (bf16[33,128,128]{2,1,0:T(8,128)(2,1)S(1)}, bf16[33,128,128]{2,1,0:T(8,128)(2,1)S(1)}, u32[]{:S(2)}, u32[]{:S(2)}) collective-permute-start(bf16[33,128,128]{2,1,0:T(8,128)(2,1)S(1)} %merge1.5), channel_id=1, source_target_pairs={{0,7},{1,0},{2,1},{3,2},{4,3},{5,4},{6,5},{7,6},{8,15},{9,8},{10,9... | collective-permute-start | bytes 3244040 | tf_op jit(solution)/shard_map/back/return1/ppermute | solution.py:305
  344.0 26.2 %collective-permute-start.16 = (bf16[33,128,128]{2,1,0:T(8,128)(2,1)S(1)}, bf16[33,128,128]{2,1,0:T(8,128)(2,1)S(1)}, u32[]{:S(2)}, u32[]{:S(2)}) collective-permute-start(bf16[33,128,128]{2,1,0:T(8,128)(2,1)S(1)} %merge0.10), channel_id=1, source_target_pairs={{0,1},{1,2},{2,3},{3,4},{4,5},{5,6},{6,7},{7,0},{8,9},{9,10},{10,1... | collective-permute-start | bytes 3244040 | tf_op jit(solution)/shard_map/back/return1/ppermute | solution.py:305
  (36 other events, 149.8 us)

commit v3 on v2

--- a/solution.py
+++ b/solution.py
@@ -210,10 +210,10 @@
 
 
 def merge_kernel(
-    j, away, arrivals, spans, info_ref, table_ref, back_ref, own_ref, own_lse_ref, *refs
+    j, away, arrivals, spans, marks, info_ref, table_ref, back_ref, own_ref, own_lse_ref, *refs
 ):
     half = info_ref[0] // 4
-    arrived, outs = refs[: len(arrivals)], refs[len(arrivals) : -2]
+    arrived, outs = refs[: len(arrivals)], refs[len(arrivals) + marks : -2]
     arrived_lse, new_lse = refs[-2:]
     tail_at = back_ref.shape[1] - 16
     for a, (low, count) in enumerate(arrivals):
@@ -276,7 +276,7 @@
             out_ref[(stop - start) * 4] = jnp.concatenate(rows, axis=0).astype(BF)
 
 
-def merge(j, away, info, table, back, own_part, arrivals, spans):
+def merge(j, away, info, table, back, own_part, arrivals, spans, mark=()):
     places = tuple((low, (acc.shape[0] - 1) // 4) for low, acc in arrivals)
     if spans is None:
         out_shape = (jax.ShapeDtypeStruct((TILES * QBLK, DH), BF),)
@@ -285,9 +285,9 @@
             jax.ShapeDtypeStruct(((stop - start) * 4 + 1, DH, QBLK), BF) for start, stop in spans
         )
     return pl.pallas_call(
-        functools.partial(merge_kernel, j, away, places, spans),
+        functools.partial(merge_kernel, j, away, places, spans, len(mark)),
         out_shape=out_shape,
-        in_specs=[SMEM, SMEM] + [VMEM] * (3 + len(arrivals)),
+        in_specs=[SMEM, SMEM] + [VMEM] * (3 + len(arrivals)) + [ANY] * len(mark),
         out_specs=(VMEM,) * len(out_shape),
         scratch_shapes=[
             pltpu.VMEM((max(1, len(arrivals)), TILES // 4, 4, QBLK), F32),
@@ -298,7 +298,33 @@
             flops=TILES * 12 * QBLK * DH, bytes_accessed=4 * 2**20, transcendentals=0
         ),
         name=f"merge{j}",
-    )(info, table, back, *own_part, *[acc for _, acc in arrivals])
+    )(info, table, back, *own_part, *[acc for _, acc in arrivals], *mark)
+
+
+def token_kernel(*refs):
+    sources, out_ref, held, sems = refs[:-3], refs[-3], refs[-2], refs[-1]
+    loads = [
+        pltpu.make_async_copy(a.at[0, 0:16, :], held.at[i], sems.at[i])
+        for i, a in enumerate(sources)
+    ]
+    for load in loads:
+        load.start()
+    for load in loads:
+        load.wait()
+    out_ref[...] = sum(held[i].astype(F32) for i in range(len(sources)))
+
+
+def token(arrays):
+    n = len(arrays)
+    return pl.pallas_call(
+        token_kernel,
+        out_shape=jax.ShapeDtypeStruct((16, DH), F32),
+        in_specs=[ANY] * n,
+        out_specs=VMEM,
+        scratch_shapes=[pltpu.VMEM((n, 16, DH), BF), pltpu.SemaphoreType.DMA((n,))],
+        compiler_params=params(),
+        name="token",
+    )(*arrays)
 
 
 def ring(x, step, axis="z", size=NZ):
@@ -387,7 +413,7 @@
         with jax.named_scope(f"own{c}"):
             return tuple(own(sources[c], CHUNKS[c], kv, info))
 
-    def merged(c, back, arrivals, spans=((0, 8),)):
+    def merged(c, back, arrivals, spans=((0, 8),), mark=()):
         out = []
         with jax.named_scope(f"merge{c}"):
             for span in spans:
@@ -397,7 +423,7 @@
                         for (at, low, high), acc in arrivals
                         if at == j and low < span[1] and high > span[0]
                     ]
-                    (acc,) = merge(j, away_by, info, table, back, owns[c], coming, (span,))
+                    (acc,) = merge(j, away_by, info, table, back, owns[c], coming, (span,), mark)
                     out.append(((j,) + span, acc))
         return out
 
@@ -426,8 +452,9 @@
         arrivals = onward(4, [((0, 0, 4), low[1]), ((1, 4, 8), high[1])])
         back2 = exchange(part2, part1, *arrays(arrivals))
         arrivals = onward(3, merged(3, back3, arrivals))
-        back1 = exchange(part1, *arrays(arrivals))
-        arrivals = onward(2, merged(2, back2, arrivals))
+        send1, mark = lax.optimization_barrier((part1, token(arrays(arrivals))))
+        back1 = exchange(send1)
+        arrivals = onward(2, merged(2, back2, arrivals, mark=(mark,)))
         back0 = exchange(part0)
         arrivals = onward(1, merged(1, back1, arrivals))
         arrivals = [(low, acc) for (_, low, _), acc in arrivals]

time: 378 us -> 369 us (0.976)
  Pallas kernels: 95.1 us -> 123 us
  waiting for transfers between devices: 131 us -> 106 us
  starting transfers between devices: 107 us -> 97.8 us
    pallas_call x5, Pallas kernels: 43.6 us -> 70.7 us  [far(): pl.pallas_call(functools.partial(far_kernel, aways, first), out_shape=jax...]
    all_to_all x9, waiting for transfers between devices: 53.2 us -> 27.8 us  [exchange(): got = lax.all_to_all(send, ('y', 'c', 'x'), 0, 0, tiled=True)]
    all_to_all x9, starting transfers between devices: 69.2 us -> 55.1 us  [exchange(): got = lax.all_to_all(send, ('y', 'c', 'x'), 0, 0, tiled=True)]
    ppermute x19, starting transfers between devices: 32.5 us -> 37.6 us  [ring(): return lax.ppermute(x, axis, [(i, (i + step) % size) for i in range(size)])]
    unnamed x83 -> x77, local copies, waits for them, and re-layouts: 33 us -> 30.3 us
    pallas_call x9 -> x10, Pallas kernels: 26.2 us -> 27.3 us  [the longest x9 27.3 us: merge(): pl.pallas_call(functools.partial(merge_kernel, j, away, places, spans, le...]
  transfers between devices with their start and end apart: 29 -> 29, of which waited for: 14 -> 11; matrix products, arithmetic and copies ran while one was open for 4% -> 4% of each run, Pallas kernels for 22% -> 30%
where the time goes in v3:
time: 369 us; the launch traced here: 367 us
  Pallas kernels  123 us (33%)
  waiting for transfers between devices  106 us (29%)
  starting transfers between devices  97.8 us (27%)
  local copies, waits for them, and re-layouts  37.5 us (10%)
    ppermute x19, waiting for transfers between devices, ring(): return lax.ppermute(x, axis, [(i, (i + step) % size) for i in range(size)])  75.1 us
    pallas_call x5, Pallas kernels, far(): pl.pallas_call(functools.partial(far_kernel, aways, first), out_shape=jax...  70.7 us
    all_to_all x9, starting transfers between devices, exchange(): got = lax.all_to_all(send, ('y', 'c', 'x'), 0, 0, tiled=True)  55.1 us
    ppermute x19, starting transfers between devices, ring(): return lax.ppermute(x, axis, [(i, (i + step) % size) for i in range(size)])  37.6 us
    unnamed x77, local copies, waits for them, and re-layouts  30.3 us
    all_to_all x9, waiting for transfers between devices, exchange(): got = lax.all_to_all(send, ('y', 'c', 'x'), 0, 0, tiled=True)  27.8 us
    pallas_call x9, Pallas kernels, merge(): pl.pallas_call(functools.partial(merge_kernel, j, away, places, spans, le...  27.3 us
    pallas_call x5, Pallas kernels, own(): pl.pallas_call(functools.partial(own_kernel, aways), out_shape=(jax.Shape...  16.9 us
  transfers between devices with their start and end apart: 29, of which 11 were waited for; matrix products, arithmetic and copies ran while one was open for 4% of the time, Pallas kernels for 30%

profile of v3, /device:TPU:1, one launch (start us, length us, event | category | flops | bytes accessed | tf_op | source)
XLA Modules:
  0.0 367.1 jit_solution(8670861157425615291)
XLA Ops:
  4.2 4.0 %collective-permute-start = (bf16[32,128,128]{2,1,0:T(8,128)(2,1)S(1)}, bf16[32,128,128]{2,1,0:T(8,128)(2,1)}, u32[]{:S(2)}, u32[]{:S(2)}) collective-permute-start(bf16[32,128,128]{2,1,0:T(8,128)(2,1)S(1)} %bitcast.52), channel_id=1, source_target_pairs={{0,7},{1,0},{2,1},{3,2},{4,3},{5,4},{6,5},{7,6},{8,15},{9,8},{10,9... | collective-permute-start | bytes 3145736 | tf_op jit(solution)/shard_map/ring1/ppermute | solution.py:331
  9.1 5.2 %all-to-all-start = ((s32[8,1,128]{2,1,0:T(1,128)}), s32[8,1,128]{2,1,0:T(1,128)S(1)}, u32[]{:S(2)}, u32[]{:S(2)}) async-start(s32[8,1,128]{2,1,0:T(1,128)} %broadcast_in_dim.61), calls=%async_computation | async-start | bytes 8192 | tf_op jit(solution)/shard_map/column/all_to_all | solution.py:350
  23.3 6.5 %copy.24 = bf16[2048,1024]{0,1:T(8,128)(2,1)} copy(bf16[2048,1024]{1,0:T(8,128)(2,1)} %param.10) | data formatting | bytes 8388608 | tf_op args[4]
  33.9 9.0 %all-to-all-start.1 = ((bf16[32,128,128]{2,1,0:T(8,128)(2,1)}), bf16[32,128,128]{2,1,0:T(8,128)(2,1)}, u32[]{:S(2)}, u32[]{:S(2)}) async-start(bf16[32,128,128]{2,1,0:T(8,128)(2,1)} %copy-done.18), calls=%async_computation.1 | async-start | bytes 2097152 | tf_op jit(solution)/shard_map/forward/all_to_all | solution.py:399
  51.2 4.3 %own2.3 = (bf16[32,128,128]{2,1,0:T(8,128)(2,1)S(1)}, f32[8,4,128]{2,1,0:T(4,128)S(1)}) custom-call(s32[128]{0:T(128)S(1)} %compare_select_fusion.5.info_ref, bf16[4,4,128,128]{3,2,1,0:T(8,128)(2,1)S(1)} %pad_maximum_fusion.kv_ref, bf16[32,128,128]{2,1,0:T(8,128)(2,1)} %collective-permute-done.refs_0_, bf16[32,128,128]{2,1,0:T(8,128)(2,1)S(1)} %collective-permute-done.1.refs_1_), custom_call_target="tpu_custom_call" | custom-call | flops 268435456 | bytes 4194304 | tf_op jit(solution)/shard_map/forward/own1/own2/pallas_call | solution.py:188
  59.0 5.5 %all-to-all-start.2 = ((s32[32,1,128]{2,1,0:T(1,128)}), s32[32,1,128]{2,1,0:T(1,128)S(1)}, u32[]{:S(2)}, u32[]{:S(2)}) async-start(s32[32,1,128]{2,1,0:T(1,128)} %bitcast.20), calls=%async_computation.2 | async-start | bytes 32768 | tf_op jit(solution)/shard_map/forward/all_to_all | solution.py:399
  64.4 4.3 %collective-permute-done.6.refs_3_.refs_1_ = bf16[32,128,128]{2,1,0:T(8,128)(2,1)} collective-permute-done((bf16[32,128,128]{2,1,0:T(8,128)(2,1)S(1)}, bf16[32,128,128]{2,1,0:T(8,128)(2,1)}, u32[]{:S(2)}, u32[]{:S(2)}) %collective-permute-start.6) | collective-permute-done | bytes 1048608 | tf_op jit(solution)/shard_map/ring2/ppermute | solution.py:331
  69.7 4.0 %pack4.1 = bf16[32,512,128]{2,1,0:T(8,128)(2,1)} custom-call(s32[256]{0:T(256)S(1)} %add_select_fusion.8.idx_ref, bf16[32,128,128]{2,1,0:T(8,128)(2,1)} %collective-permute-done.refs_0_, bf16[32,128,128]{2,1,0:T(8,128)(2,1)S(1)} %collective-permute-done.1.refs_1_, bf16[32,128,128]{2,1,0:T(8,128)(2,1)} %collective-permute-done.5.refs_2_.refs_0_, ...), custom_call_target="tpu_custom_call" | custom-call | bytes 8388608 | tf_op jit(solution)/shard_map/forward/pack4/pallas_call | solution.py:57
  73.7 8.5 %all-to-all-start.3 = ((bf16[32,512,128]{2,1,0:T(8,128)(2,1)}), bf16[32,512,128]{2,1,0:T(8,128)(2,1)}, u32[]{:S(2)}, u32[]{:S(2)}) async-start(bf16[32,512,128]{2,1,0:T(8,128)(2,1)} %pack4.1), calls=%async_computation.3 | async-start | bytes 8388608 | tf_op jit(solution)/shard_map/forward/all_to_all | solution.py:399
  85.0 23.3 %collective-permute-done.8.refs_1_ = bf16[32,128,128]{2,1,0:T(8,128)(2,1)S(1)} collective-permute-done((bf16[32,128,128]{2,1,0:T(8,128)(2,1)}, bf16[32,128,128]{2,1,0:T(8,128)(2,1)S(1)}, u32[]{:S(2)}, u32[]{:S(2)}) %collective-permute-start.8) | collective-permute-done | bytes 1048608 | tf_op jit(solution)/shard_map/ring3/ppermute | solution.py:331
  112.8 11.6 %far1.2 = bf16[32,144,128]{2,1,0:T(8,128)(2,1)} custom-call(s32[256]{0:T(256)S(1)} %reshape.340.meta_ref, bf16[32,128,128]{2,1,0:T(8,128)(2,1)} %all-to-all-done.1.got_ref, bf16[2048,1024]{1,0:T(8,128)(2,1)} %k_ref.9, bf16[1024,2048]{1,0:T(8,128)(2,1)} %bitcast.55), custom_call_target="tpu_custom_call" | custom-call | flops 1073741824 | bytes 12582912 | tf_op jit(solution)/shard_map/forward/far0/far1/pallas_call | solution.py:132
  124.4 4.7 %own2.4 = (bf16[32,128,128]{2,1,0:T(8,128)(2,1)S(1)}, f32[8,4,128]{2,1,0:T(4,128)S(1)}) custom-call(s32[128]{0:T(128)S(1)} %compare_select_fusion.5.info_ref, bf16[4,4,128,128]{3,2,1,0:T(8,128)(2,1)S(1)} %pad_maximum_fusion.kv_ref, bf16[32,128,128]{2,1,0:T(8,128)(2,1)} %collective-permute-done.5.refs_2_.refs_0_, ...), custom_call_target="tpu_custom_call" | custom-call | flops 268435456 | bytes 4194304 | tf_op jit(solution)/shard_map/forward/own2/own2/pallas_call | solution.py:188
  133.8 5.2 %all-to-all-start.4 = ((bf16[32,384,128]{2,1,0:T(8,128)(2,1)}), bf16[32,384,128]{2,1,0:T(8,128)(2,1)S(1)}, u32[]{:S(2)}, u32[]{:S(2)}) async-start(bf16[32,384,128]{2,1,0:T(8,128)(2,1)} %pack3.1), calls=%async_computation.4 | async-start | bytes 6291456 | tf_op jit(solution)/shard_map/forward/all_to_all | solution.py:399
  149.1 16.6 %far2.5 = bf16[32,272,128]{2,1,0:T(8,128)(2,1)S(1)} custom-call(s32[256]{0:T(256)S(1)} %reshape.340.meta_ref, bf16[32,512,128]{2,1,0:T(8,128)(2,1)} %all-to-all-done.3.got_ref, bf16[2048,1024]{1,0:T(8,128)(2,1)} %k_ref.9, bf16[1024,2048]{1,0:T(8,128)(2,1)} %bitcast.56), custom_call_target="tpu_custom_call" | custom-call | flops 2147483648 | bytes 12582912 | tf_op jit(solution)/shard_map/forward/far2/far2/pallas_call | solution.py:132
  167.1 9.9 %all-to-all-done.4.got_ref = bf16[32,384,128]{2,1,0:T(8,128)(2,1)S(1)} async-done(((bf16[32,384,128]{2,1,0:T(8,128)(2,1)}), bf16[32,384,128]{2,1,0:T(8,128)(2,1)S(1)}, u32[]{:S(2)}, u32[]{:S(2)}) %all-to-all-start.4) | async-done | bytes 3145760 | tf_op jit(solution)/shard_map/forward/all_to_all | solution.py:399
  176.9 9.8 %far1.3 = bf16[32,144,128]{2,1,0:T(8,128)(2,1)S(1)} custom-call(s32[256]{0:T(256)S(1)} %reshape.340.meta_ref, bf16[32,384,128]{2,1,0:T(8,128)(2,1)S(1)} %all-to-all-done.4.got_ref, bf16[2048,1024]{1,0:T(8,128)(2,1)} %k_ref.9, bf16[1024,2048]{1,0:T(8,128)(2,1)} %bitcast.57), custom_call_target="tpu_custom_call" | custom-call | flops 1073741824 | bytes 12582912 | tf_op jit(solution)/shard_map/forward/far4/far1/pallas_call | solution.py:132
  187.8 4.4 %all-to-all-start.5 = ((bf16[32,144,128]{2,1,0:T(8,128)(2,1)}), bf16[32,144,128]{2,1,0:T(8,128)(2,1)}, u32[]{:S(2)}, u32[]{:S(2)}) async-start(bf16[32,144,128]{2,1,0:T(8,128)(2,1)} %copy-done.11), calls=%async_computation.5 | async-start | bytes 2359296 | tf_op jit(solution)/shard_map/back/all_to_all | solution.py:399
  192.2 16.1 %far2.4 = bf16[32,272,128]{2,1,0:T(8,128)(2,1)S(1)} custom-call(s32[256]{0:T(256)S(1)} %reshape.340.meta_ref, bf16[32,384,128]{2,1,0:T(8,128)(2,1)S(1)} %all-to-all-done.4.got_ref, bf16[2048,1024]{1,0:T(8,128)(2,1)} %k_ref.9, bf16[1024,2048]{1,0:T(8,128)(2,1)} %bitcast.58), custom_call_target="tpu_custom_call" | custom-call | flops 2147483648 | bytes 12582912 | tf_op jit(solution)/shard_map/forward/far3/far2/pallas_call | solution.py:132
  209.9 4.0 %all-to-all-start.6 = ((bf16[32,272,128]{2,1,0:T(8,128)(2,1)}), bf16[32,272,128]{2,1,0:T(8,128)(2,1)S(1)}, u32[]{:S(2)}, u32[]{:S(2)}) async-start(bf16[32,272,128]{2,1,0:T(8,128)(2,1)} %copy-done.2), calls=%async_computation.6 | async-start | bytes 4456448 | tf_op jit(solution)/shard_map/back/all_to_all | solution.py:399
  215.8 6.5 %collective-permute-start.11 = (bf16[17,128,128]{2,1,0:T(8,128)(2,1)S(1)}, bf16[17,128,128]{2,1,0:T(8,128)(2,1)S(1)}, u32[]{:S(2)}, u32[]{:S(2)}) collective-permute-start(bf16[17,128,128]{2,1,0:T(8,128)(2,1)S(1)} %merge0.6), channel_id=1, source_target_pairs={{0,1},{1,2},{2,3},{3,4},{4,5},{5,6},{6,7},{7,0},{8,9},{9,10},{10,1... | collective-permute-start | bytes 1671176 | tf_op jit(solution)/shard_map/back/return4/ppermute | solution.py:331
  224.3 16.6 %far2.3 = bf16[32,272,128]{2,1,0:T(8,128)(2,1)S(1)} custom-call(s32[256]{0:T(256)S(1)} %reshape.340.meta_ref, bf16[32,512,128]{2,1,0:T(8,128)(2,1)} %all-to-all-done.3.got_ref, bf16[2048,1024]{1,0:T(8,128)(2,1)} %k_ref.9, bf16[1024,2048]{1,0:T(8,128)(2,1)} %bitcast.59), custom_call_target="tpu_custom_call" | custom-call | flops 2147483648 | bytes 12582912 | tf_op jit(solution)/shard_map/forward/far1/far2/pallas_call | solution.py:132
  243.9 4.6 %all-to-all-start.7 = ((bf16[32,272,128]{2,1,0:T(8,128)(2,1)}), bf16[32,272,128]{2,1,0:T(8,128)(2,1)}, u32[]{:S(2)}, u32[]{:S(2)}) async-start(bf16[32,272,128]{2,1,0:T(8,128)(2,1)} %copy-done.3), calls=%async_computation.7 | async-start | bytes 4456448 | tf_op jit(solution)/shard_map/back/all_to_all | solution.py:399
  251.9 5.5 %collective-permute-start.12 = (bf16[33,128,128]{2,1,0:T(8,128)(2,1)S(1)}, bf16[33,128,128]{2,1,0:T(8,128)(2,1)S(1)}, u32[]{:S(2)}, u32[]{:S(2)}) collective-permute-start(bf16[33,128,128]{2,1,0:T(8,128)(2,1)S(1)} %merge0.7), channel_id=1, source_target_pairs={{0,1},{1,2},{2,3},{3,4},{4,5},{5,6},{6,7},{7,0},{8,9},{9,10},{10,1... | collective-permute-start | bytes 3244040 | tf_op jit(solution)/shard_map/back/return3/ppermute | solution.py:331
  260.1 20.3 %collective-permute-done.12.refs_0_ = bf16[33,128,128]{2,1,0:T(8,128)(2,1)S(1)} collective-permute-done((bf16[33,128,128]{2,1,0:T(8,128)(2,1)S(1)}, bf16[33,128,128]{2,1,0:T(8,128)(2,1)S(1)}, u32[]{:S(2)}, u32[]{:S(2)}) %collective-permute-start.12) | collective-permute-done | bytes 1081376 | tf_op jit(solution)/shard_map/back/return3/ppermute | solution.py:331
  280.4 4.6 %collective-permute-done.14.refs_1_.refs_0_ = bf16[33,128,128]{2,1,0:T(8,128)(2,1)S(1)} collective-permute-done((bf16[33,128,128]{2,1,0:T(8,128)(2,1)S(1)}, bf16[33,128,128]{2,1,0:T(8,128)(2,1)S(1)}, u32[]{:S(2)}, u32[]{:S(2)}) %collective-permute-start.14) | collective-permute-done | bytes 1081376 | tf_op jit(solution)/shard_map/back/return3/ppermute | solution.py:331
  286.1 8.4 %all-to-all-start.8 = ((bf16[32,272,128]{2,1,0:T(8,128)(2,1)}), bf16[32,272,128]{2,1,0:T(8,128)(2,1)S(1)}, u32[]{:S(2)}, u32[]{:S(2)}) async-start(bf16[32,272,128]{2,1,0:T(8,128)(2,1)} %copy-done.4), calls=%async_computation.8 | async-start | bytes 4456448 | tf_op jit(solution)/shard_map/back/all_to_all | solution.py:399
  295.8 4.4 %merge0.9 = bf16[33,128,128]{2,1,0:T(8,128)(2,1)} custom-call(s32[128]{0:T(128)S(1)} %compare_select_fusion.5.info_ref, s32[1024]{0:T(1024)S(1)} %fusion.18.table_ref, bf16[32,272,128]{2,1,0:T(8,128)(2,1)} %all-to-all-done.7.back_ref, bf16[32,128,128]{2,1,0:T(8,128)(2,1)S(1)} %copy-done.17, f32[8,4,128]{2,1,0:T(4,128)S(1)} %get-tuple-element.43.own_lse_ref, ...), custom_call_target="tpu_custom_call" | custom-call | flops 6291456 | bytes 4194304 | tf_op jit(solution)/shard_map/back/merge2/merge0/pallas_call | solution.py:287
  300.2 4.5 %merge1.4 = bf16[33,128,128]{2,1,0:T(8,128)(2,1)} custom-call(s32[128]{0:T(128)S(1)} %compare_select_fusion.5.info_ref, s32[1024]{0:T(1024)S(1)} %fusion.18.table_ref, bf16[32,272,128]{2,1,0:T(8,128)(2,1)} %all-to-all-done.7.back_ref, bf16[32,128,128]{2,1,0:T(8,128)(2,1)S(1)} %copy-done.17, f32[8,4,128]{2,1,0:T(4,128)S(1)} %get-tuple-element.43.own_lse_ref, ...), custom_call_target="tpu_custom_call" | custom-call | flops 6291456 | bytes 4194304 | tf_op jit(solution)/shard_map/back/merge2/merge1/pallas_call | solution.py:287
  307.4 15.4 %all-to-all-done.8.back_ref = bf16[32,272,128]{2,1,0:T(8,128)(2,1)S(1)} async-done(((bf16[32,272,128]{2,1,0:T(8,128)(2,1)}), bf16[32,272,128]{2,1,0:T(8,128)(2,1)S(1)}, u32[]{:S(2)}, u32[]{:S(2)}) %all-to-all-start.8) | async-done | bytes 2228256 | tf_op jit(solution)/shard_map/back/all_to_all | solution.py:399
  322.8 5.5 %all-to-all-start.9 = ((bf16[32,144,128]{2,1,0:T(8,128)(2,1)}), bf16[32,144,128]{2,1,0:T(8,128)(2,1)S(1)}, u32[]{:S(2)}, u32[]{:S(2)}) async-start(bf16[32,144,128]{2,1,0:T(8,128)(2,1)} %far1.2), calls=%async_computation.9 | async-start | bytes 2359296 | tf_op jit(solution)/shard_map/back/all_to_all | solution.py:399
  338.3 20.7 %collective-permute-done.16.refs_0_ = bf16[33,128,128]{2,1,0:T(8,128)(2,1)S(1)} collective-permute-done((bf16[33,128,128]{2,1,0:T(8,128)(2,1)S(1)}, bf16[33,128,128]{2,1,0:T(8,128)(2,1)S(1)}, u32[]{:S(2)}, u32[]{:S(2)}) %collective-permute-start.16) | collective-permute-done | bytes 1081376 | tf_op jit(solution)/shard_map/back/return1/ppermute | solution.py:331
  363.3 3.9 %merge0.11 = bf16[4096,128]{1,0:T(8,128)(2,1)} custom-call(s32[128]{0:T(128)S(1)} %compare_select_fusion.5.info_ref, s32[1024]{0:T(1024)S(1)} %fusion.18.table_ref, bf16[32,144,128]{2,1,0:T(8,128)(2,1)S(1)} %all-to-all-done.9.back_ref, bf16[16,128,128]{2,1,0:T(8,128)(2,1)S(1)} %copy-done.31, f32[4,4,128]{2,1,0:T(4,128)S(1)} %get-tuple-element.36.own_lse_ref, ...), custom_call_target="tpu_custom_call" | custom-call | flops 6291456 | bytes 4194304 | tf_op jit(solution)/shard_map/back/merge0/pallas_call | solution.py:287
  (157 shorter events, 88.8 us)
Async XLA Ops:
  1.7 32.2 %collective-permute-start.1 = (bf16[32,128,128]{2,1,0:T(8,128)(2,1)S(1)}, bf16[32,128,128]{2,1,0:T(8,128)(2,1)S(1)}, u32[]{:S(2)}, u32[]{:S(2)}) collective-permute-start(bf16[32,128,128]{2,1,0:T(8,128)(2,1)S(1)} %bitcast.51), channel_id=1, source_target_pairs={{0,1},{1,2},{2,3},{3,4},{4,5},{5,6},{6,7},{7,0},{8,9},{9,10},{10,1... | collective-permute-start | bytes 3145736 | tf_op jit(solution)/shard_map/ring1/ppermute | solution.py:331
  4.2 29.6 %collective-permute-start = (bf16[32,128,128]{2,1,0:T(8,128)(2,1)S(1)}, bf16[32,128,128]{2,1,0:T(8,128)(2,1)}, u32[]{:S(2)}, u32[]{:S(2)}) collective-permute-start(bf16[32,128,128]{2,1,0:T(8,128)(2,1)S(1)} %bitcast.52), channel_id=1, source_target_pairs={{0,7},{1,0},{2,1},{3,2},{4,3},{5,4},{6,5},{7,6},{8,15},{9,8},{10,9... | collective-permute-start | bytes 3145736 | tf_op jit(solution)/shard_map/ring1/ppermute | solution.py:331
  9.1 23.5 %all-to-all-start = ((s32[8,1,128]{2,1,0:T(1,128)}), s32[8,1,128]{2,1,0:T(1,128)S(1)}, u32[]{:S(2)}, u32[]{:S(2)}) async-start(s32[8,1,128]{2,1,0:T(1,128)} %broadcast_in_dim.61), calls=%async_computation | async-start | bytes 8192 | tf_op jit(solution)/shard_map/column/all_to_all | solution.py:350
  14.9 31.7 %collective-permute-start.2 = (bf16[4,128,128]{2,1,0:T(8,128)(2,1)S(1)}, bf16[4,128,128]{2,1,0:T(8,128)(2,1)S(1)}, u32[]{:S(2)}, u32[]{:S(2)}) collective-permute-start(bf16[4,128,128]{2,1,0:T(8,128)(2,1)S(1)} %get-tuple-element.60), channel_id=1, source_target_pairs={{0,8},{8,16},{16,24},{24,0},{1,9},{9,17},{17,25},{25,1},{2,10},{10... | collective-permute-start | bytes 393224 | tf_op jit(solution)/shard_map/kv/ppermute | solution.py:331
  16.2 30.4 %collective-permute-start.3 = (bf16[4,128,128]{2,1,0:T(8,128)(2,1)S(1)}, bf16[4,128,128]{2,1,0:T(8,128)(2,1)S(1)}, u32[]{:S(2)}, u32[]{:S(2)}) collective-permute-start(bf16[4,128,128]{2,1,0:T(8,128)(2,1)S(1)} %get-tuple-element.61), channel_id=1, source_target_pairs={{0,16},{8,24},{16,0},{24,8},{1,17},{9,25},{17,1},{25,9},{2,18},{10... | collective-permute-start | bytes 393224 | tf_op jit(solution)/shard_map/kv/ppermute | solution.py:331
  18.6 28.0 %collective-permute-start.4 = (bf16[4,128,128]{2,1,0:T(8,128)(2,1)S(1)}, bf16[4,128,128]{2,1,0:T(8,128)(2,1)S(1)}, u32[]{:S(2)}, u32[]{:S(2)}) collective-permute-start(bf16[4,128,128]{2,1,0:T(8,128)(2,1)S(1)} %get-tuple-element.62), channel_id=1, source_target_pairs={{0,24},{8,0},{16,8},{24,16},{1,25},{9,1},{17,9},{25,17},{2,26},{10... | collective-permute-start | bytes 393224 | tf_op jit(solution)/shard_map/kv/ppermute | solution.py:331
  33.9 25.1 %all-to-all-start.1 = ((bf16[32,128,128]{2,1,0:T(8,128)(2,1)}), bf16[32,128,128]{2,1,0:T(8,128)(2,1)}, u32[]{:S(2)}, u32[]{:S(2)}) async-start(bf16[32,128,128]{2,1,0:T(8,128)(2,1)} %copy-done.18), calls=%async_computation.1 | async-start | bytes 2097152 | tf_op jit(solution)/shard_map/forward/all_to_all | solution.py:399
  42.9 25.8 %collective-permute-start.6 = (bf16[32,128,128]{2,1,0:T(8,128)(2,1)S(1)}, bf16[32,128,128]{2,1,0:T(8,128)(2,1)}, u32[]{:S(2)}, u32[]{:S(2)}) collective-permute-start(bf16[32,128,128]{2,1,0:T(8,128)(2,1)S(1)} %collective-permute-done.1.refs_1_), channel_id=1, source_target_pairs={{0,1},{1,2},{2,3},{3,4},{4,5},{5,6},{6,7},{7,0},{8,9},{9,10},{10,1... | collective-permute-start | bytes 3145736 | tf_op jit(solution)/shard_map/ring2/ppermute | solution.py:331
  45.2 24.4 %collective-permute-start.5 = (bf16[32,128,128]{2,1,0:T(8,128)(2,1)}, bf16[32,128,128]{2,1,0:T(8,128)(2,1)}, u32[]{:S(2)}, u32[]{:S(2)}) collective-permute-start(bf16[32,128,128]{2,1,0:T(8,128)(2,1)} %collective-permute-done.refs_0_), channel_id=1, source_target_pairs={{0,7},{1,0},{2,1},{3,2},{4,3},{5,4},{6,5},{7,6},{8,15},{9,8},{10,9... | collective-permute-start | bytes 3145736 | tf_op jit(solution)/shard_map/ring2/ppermute | solution.py:331
  48.3 76.1 %copy-start = (bf16[4,4,128,128]{3,2,1,0:T(8,128)(2,1)}, bf16[4,4,128,128]{3,2,1,0:T(8,128)(2,1)S(1)}, u32[]{:S(2)}) copy-start(bf16[4,4,128,128]{3,2,1,0:T(8,128)(2,1)S(1)} %pad_maximum_fusion.kv_ref) | copy-start | bytes 1572868
  59.0 14.7 %all-to-all-start.2 = ((s32[32,1,128]{2,1,0:T(1,128)}), s32[32,1,128]{2,1,0:T(1,128)S(1)}, u32[]{:S(2)}, u32[]{:S(2)}) async-start(s32[32,1,128]{2,1,0:T(1,128)} %bitcast.20), calls=%async_computation.2 | async-start | bytes 32768 | tf_op jit(solution)/shard_map/forward/all_to_all | solution.py:399
  73.7 60.1 %all-to-all-start.3 = ((bf16[32,512,128]{2,1,0:T(8,128)(2,1)}), bf16[32,512,128]{2,1,0:T(8,128)(2,1)}, u32[]{:S(2)}, u32[]{:S(2)}) async-start(bf16[32,512,128]{2,1,0:T(8,128)(2,1)} %pack4.1), calls=%async_computation.3 | async-start | bytes 8388608 | tf_op jit(solution)/shard_map/forward/all_to_all | solution.py:399
  82.2 26.0 %collective-permute-start.8 = (bf16[32,128,128]{2,1,0:T(8,128)(2,1)}, bf16[32,128,128]{2,1,0:T(8,128)(2,1)S(1)}, u32[]{:S(2)}, u32[]{:S(2)}) collective-permute-start(bf16[32,128,128]{2,1,0:T(8,128)(2,1)} %collective-permute-done.6.refs_3_.refs_1_), channel_id=1, source_target_pairs={{0,1},{1,2},{2,3},{3,4},{4,5},{5,6},{6,7},{7,0},{8,9},{9,10},{10,1... | collective-permute-start | bytes 3145736 | tf_op jit(solution)/shard_map/ring3/ppermute | solution.py:331
  82.6 26.6 %collective-permute-start.7 = (bf16[32,128,128]{2,1,0:T(8,128)(2,1)}, bf16[32,128,128]{2,1,0:T(8,128)(2,1)S(1)}, u32[]{:S(2)}, u32[]{:S(2)}) collective-permute-start(bf16[32,128,128]{2,1,0:T(8,128)(2,1)} %collective-permute-done.5.refs_2_.refs_0_), channel_id=1, source_target_pairs={{0,7},{1,0},{2,1},{3,2},{4,3},{5,4},{6,5},{7,6},{8,15},{9,8},{10,9... | collective-permute-start | bytes 3145736 | tf_op jit(solution)/shard_map/ring3/ppermute | solution.py:331
  108.2 22.3 %copy-start.5 = (bf16[32,128,128]{2,1,0:T(8,128)(2,1)}, bf16[32,128,128]{2,1,0:T(8,128)(2,1)S(1)}, u32[]{:S(2)}) copy-start(bf16[32,128,128]{2,1,0:T(8,128)(2,1)S(1)} %collective-permute-done.8.refs_1_) | copy-start | bytes 3145732
  109.2 19.9 %collective-permute-start.9 = (bf16[16,128,128]{2,1,0:T(8,128)(2,1)}, bf16[16,128,128]{2,1,0:T(8,128)(2,1)S(1)}, u32[]{:S(2)}, u32[]{:S(2)}) collective-permute-start(bf16[16,128,128]{2,1,0:T(8,128)(2,1)} %slice.15), channel_id=1, source_target_pairs={{0,1},{1,2},{2,3},{3,4},{4,5},{5,6},{6,7},{7,0},{8,9},{9,10},{10,1... | collective-permute-start | bytes 1572872 | tf_op jit(solution)/shard_map/ring4/ppermute | solution.py:331
  109.2 21.4 %copy-start.7 = (bf16[32,128,128]{2,1,0:T(8,128)(2,1)}, bf16[32,128,128]{2,1,0:T(8,128)(2,1)S(1)}, u32[]{:S(2)}) copy-start(bf16[32,128,128]{2,1,0:T(8,128)(2,1)S(1)} %collective-permute-done.7.refs_0_) | copy-start | bytes 3145732
  110.1 19.1 %collective-permute-start.10 = (bf16[16,128,128]{2,1,0:T(8,128)(2,1)}, bf16[16,128,128]{2,1,0:T(8,128)(2,1)}, u32[]{:S(2)}, u32[]{:S(2)}) collective-permute-start(bf16[16,128,128]{2,1,0:T(8,128)(2,1)} %slice.16), channel_id=1, source_target_pairs={{0,7},{1,0},{2,1},{3,2},{4,3},{5,4},{6,5},{7,6},{8,15},{9,8},{10,9... | collective-permute-start | bytes 1572872 | tf_op jit(solution)/shard_map/ring4/ppermute | solution.py:331
  133.8 43.1 %all-to-all-start.4 = ((bf16[32,384,128]{2,1,0:T(8,128)(2,1)}), bf16[32,384,128]{2,1,0:T(8,128)(2,1)S(1)}, u32[]{:S(2)}, u32[]{:S(2)}) async-start(bf16[32,384,128]{2,1,0:T(8,128)(2,1)} %pack3.1), calls=%async_computation.4 | async-start | bytes 6291456 | tf_op jit(solution)/shard_map/forward/all_to_all | solution.py:399
  187.8 22.1 %all-to-all-start.5 = ((bf16[32,144,128]{2,1,0:T(8,128)(2,1)}), bf16[32,144,128]{2,1,0:T(8,128)(2,1)}, u32[]{:S(2)}, u32[]{:S(2)}) async-start(bf16[32,144,128]{2,1,0:T(8,128)(2,1)} %copy-done.11), calls=%async_computation.5 | async-start | bytes 2359296 | tf_op jit(solution)/shard_map/back/all_to_all | solution.py:399
  209.9 34.1 %all-to-all-start.6 = ((bf16[32,272,128]{2,1,0:T(8,128)(2,1)}), bf16[32,272,128]{2,1,0:T(8,128)(2,1)S(1)}, u32[]{:S(2)}, u32[]{:S(2)}) async-start(bf16[32,272,128]{2,1,0:T(8,128)(2,1)} %copy-done.2), calls=%async_computation.6 | async-start | bytes 4456448 | tf_op jit(solution)/shard_map/back/all_to_all | solution.py:399
  215.8 25.1 %collective-permute-start.11 = (bf16[17,128,128]{2,1,0:T(8,128)(2,1)S(1)}, bf16[17,128,128]{2,1,0:T(8,128)(2,1)S(1)}, u32[]{:S(2)}, u32[]{:S(2)}) collective-permute-start(bf16[17,128,128]{2,1,0:T(8,128)(2,1)S(1)} %merge0.6), channel_id=1, source_target_pairs={{0,1},{1,2},{2,3},{3,4},{4,5},{5,6},{6,7},{7,0},{8,9},{9,10},{10,1... | collective-permute-start | bytes 1671176 | tf_op jit(solution)/shard_map/back/return4/ppermute | solution.py:331
  224.3 18.9 %collective-permute-start.13 = (bf16[17,128,128]{2,1,0:T(8,128)(2,1)S(1)}, bf16[17,128,128]{2,1,0:T(8,128)(2,1)S(1)}, u32[]{:S(2)}, u32[]{:S(2)}) collective-permute-start(bf16[17,128,128]{2,1,0:T(8,128)(2,1)S(1)} %merge0.8), channel_id=1, source_target_pairs={{0,7},{1,0},{2,1},{3,2},{4,3},{5,4},{6,5},{7,6},{8,15},{9,8},{10,9... | collective-permute-start | bytes 1671176 | tf_op jit(solution)/shard_map/back/return4/ppermute | solution.py:331
  243.9 42.2 %all-to-all-start.7 = ((bf16[32,272,128]{2,1,0:T(8,128)(2,1)}), bf16[32,272,128]{2,1,0:T(8,128)(2,1)}, u32[]{:S(2)}, u32[]{:S(2)}) async-start(bf16[32,272,128]{2,1,0:T(8,128)(2,1)} %copy-done.3), calls=%async_computation.7 | async-start | bytes 4456448 | tf_op jit(solution)/shard_map/back/all_to_all | solution.py:399
  251.9 28.5 %collective-permute-start.12 = (bf16[33,128,128]{2,1,0:T(8,128)(2,1)S(1)}, bf16[33,128,128]{2,1,0:T(8,128)(2,1)S(1)}, u32[]{:S(2)}, u32[]{:S(2)}) collective-permute-start(bf16[33,128,128]{2,1,0:T(8,128)(2,1)S(1)} %merge0.7), channel_id=1, source_target_pairs={{0,1},{1,2},{2,3},{3,4},{4,5},{5,6},{6,7},{7,0},{8,9},{9,10},{10,1... | collective-permute-start | bytes 3244040 | tf_op jit(solution)/shard_map/back/return3/ppermute | solution.py:331
  259.8 25.1 %collective-permute-start.14 = (bf16[33,128,128]{2,1,0:T(8,128)(2,1)S(1)}, bf16[33,128,128]{2,1,0:T(8,128)(2,1)S(1)}, u32[]{:S(2)}, u32[]{:S(2)}) collective-permute-start(bf16[33,128,128]{2,1,0:T(8,128)(2,1)S(1)} %merge1.3), channel_id=1, source_target_pairs={{0,7},{1,0},{2,1},{3,2},{4,3},{5,4},{6,5},{7,6},{8,15},{9,8},{10,9... | collective-permute-start | bytes 3244040 | tf_op jit(solution)/shard_map/back/return3/ppermute | solution.py:331
  286.1 36.7 %all-to-all-start.8 = ((bf16[32,272,128]{2,1,0:T(8,128)(2,1)}), bf16[32,272,128]{2,1,0:T(8,128)(2,1)S(1)}, u32[]{:S(2)}, u32[]{:S(2)}) async-start(bf16[32,272,128]{2,1,0:T(8,128)(2,1)} %copy-done.4), calls=%async_computation.8 | async-start | bytes 4456448 | tf_op jit(solution)/shard_map/back/all_to_all | solution.py:399
  300.2 28.1 %collective-permute-start.15 = (bf16[33,128,128]{2,1,0:T(8,128)(2,1)}, bf16[33,128,128]{2,1,0:T(8,128)(2,1)}, u32[]{:S(2)}, u32[]{:S(2)}) collective-permute-start(bf16[33,128,128]{2,1,0:T(8,128)(2,1)} %merge0.9), channel_id=1, source_target_pairs={{0,1},{1,2},{2,3},{3,4},{4,5},{5,6},{6,7},{7,0},{8,9},{9,10},{10,1... | collective-permute-start | bytes 3244040 | tf_op jit(solution)/shard_map/back/return2/ppermute | solution.py:331
  304.7 27.9 %collective-permute-start.17 = (bf16[33,128,128]{2,1,0:T(8,128)(2,1)}, bf16[33,128,128]{2,1,0:T(8,128)(2,1)}, u32[]{:S(2)}, u32[]{:S(2)}) collective-permute-start(bf16[33,128,128]{2,1,0:T(8,128)(2,1)} %merge1.4), channel_id=1, source_target_pairs={{0,7},{1,0},{2,1},{3,2},{4,3},{5,4},{6,5},{7,6},{8,15},{9,8},{10,9... | collective-permute-start | bytes 3244040 | tf_op jit(solution)/shard_map/back/return2/ppermute | solution.py:331
  322.8 38.2 %all-to-all-start.9 = ((bf16[32,144,128]{2,1,0:T(8,128)(2,1)}), bf16[32,144,128]{2,1,0:T(8,128)(2,1)S(1)}, u32[]{:S(2)}, u32[]{:S(2)}) async-start(bf16[32,144,128]{2,1,0:T(8,128)(2,1)} %far1.2), calls=%async_computation.9 | async-start | bytes 2359296 | tf_op jit(solution)/shard_map/back/all_to_all | solution.py:399
  332.5 26.5 %collective-permute-start.16 = (bf16[33,128,128]{2,1,0:T(8,128)(2,1)S(1)}, bf16[33,128,128]{2,1,0:T(8,128)(2,1)S(1)}, u32[]{:S(2)}, u32[]{:S(2)}) collective-permute-start(bf16[33,128,128]{2,1,0:T(8,128)(2,1)S(1)} %merge0.10), channel_id=1, source_target_pairs={{0,1},{1,2},{2,3},{3,4},{4,5},{5,6},{6,7},{7,0},{8,9},{9,10},{10,1... | collective-permute-start | bytes 3244040 | tf_op jit(solution)/shard_map/back/return1/ppermute | solution.py:331
  335.5 25.4 %collective-permute-start.18 = (bf16[33,128,128]{2,1,0:T(8,128)(2,1)S(1)}, bf16[33,128,128]{2,1,0:T(8,128)(2,1)S(1)}, u32[]{:S(2)}, u32[]{:S(2)}) collective-permute-start(bf16[33,128,128]{2,1,0:T(8,128)(2,1)S(1)} %merge1.5), channel_id=1, source_target_pairs={{0,7},{1,0},{2,1},{3,2},{4,3},{5,4},{6,5},{7,6},{8,15},{9,8},{10,9... | collective-permute-start | bytes 3244040 | tf_op jit(solution)/shard_map/back/return1/ppermute | solution.py:331
  (33 other events, 99.7 us)
